TPU v7x, 512 devices: a whole 4x4x16 slice. The times are simulated.
512 devices in a mesh: fsdp: 64 (over y, z_hi, x, core), basis: 8 (over z_lo).
Axes of the slice: x: 4, y: 4, z: 16 (z_hi: 2, z_lo: 8; z = z_hi * 8 + z_lo), core: 2. Of those that a mesh axis runs over, the one named last changes fastest.
Arguments:
- activations: bfloat16 [2048, 6144], P('basis', 'fsdp'), may hold values from -6 to 6
- hidden_grad: bfloat16 [2048, 8192], P('basis', 'fsdp'), may hold values from -0.1796875 to 0.1796875
- block_rows: int32 [16], P('basis'), may hold values from 1 to 128, 1280 in all
- basis: bfloat16 [6144, 4096], P('fsdp', 'basis'), may hold values from -0.21875 to 0.21875
- accumulated: float32 [6144, 8192], P('basis', 'fsdp'), may hold values from -3 to 3
Outputs:
- projected: float32 [6144, 8192], P('basis', 'fsdp')
Inputs may be any that keep to these rules, and one draw needn't show every extreme that they name: `block_rows`: every block holds at least one routed token, and some block is full.
All inputs are finite; a program needn't handle non-finite values.
Results may differ from a plain program's by a relative error of at most 0.029.
Values may be sent and summed in bfloat16 or wider, within the bound.
No kernel may reach another device: no remote copies, remote signals or barrier semaphores. Data moves between devices by JAX's collectives and lax.ppermute only.
A program may use at most 64 MiB of HBM per device.

v0:
```python
import jax
import jax.numpy as jnp
from jax import lax
from jax.sharding import PartitionSpec as P

BLOCK = 128


def on_device(activations, hidden_grad, block_rows, basis, accumulated):
    block_size = BLOCK
    tok_count = activations.shape[0]
    blocks_here = block_rows.shape[0]
    position = jnp.arange(tok_count, dtype=jnp.int32)
    block_index = position // block_size
    fill_count = jnp.sum(
        jnp.where(
            block_index[:, None] == jnp.arange(blocks_here, dtype=jnp.int32)[None, :],
            block_rows[None, :],
            0,
        ),
        axis=1,
    )
    live_rows = position % block_size < fill_count
    masked = jnp.where(live_rows[:, None], hidden_grad, jnp.zeros_like(hidden_grad))
    features = lax.all_gather(activations, "fsdp", axis=1, tiled=True)
    partial_value = lax.dot_general(
        features, masked, (((0,), (0,)), ((), ())), preferred_element_type=jnp.float32
    )
    row_count = partial_value.shape[0] // lax.axis_size("basis")
    row_start = lax.axis_index("basis") * row_count
    current = lax.dynamic_slice_in_dim(partial_value, row_start, row_count, 0)
    partial_value = lax.dynamic_update_slice_in_dim(
        partial_value, current + accumulated, row_start, 0
    )
    gradient = lax.psum(partial_value.astype(jnp.bfloat16), "basis")
    own_rows = lax.dynamic_slice_in_dim(gradient, row_start, row_count, 0)
    panel_full = lax.all_gather(basis, "fsdp", axis=0, tiled=True)
    coeff_sum = lax.dot_general(
        panel_full, gradient, (((0,), (0,)), ((), ())), preferred_element_type=jnp.float32
    )
    coeffs = coeff_sum.astype(jnp.bfloat16)
    removal_part = jnp.dot(panel_full, coeffs, preferred_element_type=jnp.float32)
    removed = lax.psum_scatter(
        removal_part.astype(jnp.bfloat16), "basis", scatter_dimension=0, tiled=True
    ).astype(jnp.float32)
    return own_rows.astype(jnp.float32) - removed


def solution(mesh):
    placed = (
        P("basis", "fsdp"),
        P("basis", "fsdp"),
        P("basis"),
        P("fsdp", "basis"),
        P("basis", "fsdp"),
    )
    return jax.shard_map(
        on_device, mesh=mesh, in_specs=placed, out_specs=P("basis", "fsdp"), check_vma=False
    )
```

profile of v0, /device:TPU:1, one launch (start us, length us, event | category | flops | bytes accessed | tf_op | source)
XLA Modules:
  0.0 491.9 jit_solution(16144019380713073946)
XLA Ops:
  6.5 0.0 all-gather.3.cloned.1.call-start
  6.5 0.7 all-gather.3.cloned.1.call-update
  7.3 0.0 all-reduce.2.cloned.1.call-start
  7.3 1.2 copy.8
  8.5 0.7 fusion.6
  9.2 130.7 %all-gather.3.cloned.1.call-done = bf16[256,6144]{0,1:T(8,128)(2,1)} async-done(((bf16[256,96]{0,1:T(8,128)(2,1)}), bf16[256,6144]{0,1:T(8,128)(2,1)}) %all-gather.3.cloned.1.call-update) | async-done | bytes 3145744 | tf_op jit(solution)/shard_map/all_gather | solution.py:25
  139.9 3.2 fusion.2
  143.1 0.3 copy.10
  143.4 0.1 fusion.1
  143.4 1.4 convert_element_type.19
  144.8 0.0 all-reduce.2.cloned.1.call-update
  144.9 0.0 all-gather.5.cloned.1.call-start
  144.9 0.7 all-gather.5.cloned.1.call-update
  145.6 0.0 reduce-scatter.2.cloned.1.call-start
  145.6 115.7 %all-reduce.2.cloned.1.call-done = bf16[6144,128]{0,1:T(8,128)(2,1)} async-done(((bf16[6144,128]{0,1:T(8,128)(2,1)}), bf16[6144,128]{0,1:T(8,128)(2,1)}) %all-reduce.2.cloned.1.call-update) | async-done | bytes 1572880 | tf_op jit(solution)/shard_map/psum | solution.py:35
  261.3 155.2 %all-gather.5.cloned.1.call-done = bf16[6144,512]{1,0:T(8,128)(2,1)} async-done(((bf16[96,512]{1,0:T(8,128)(2,1)}), bf16[6144,512]{1,0:T(8,128)(2,1)}) %all-gather.5.cloned.1.call-update) | async-done | bytes 6291472 | tf_op jit(solution)/shard_map/all_gather | solution.py:37
  416.5 9.3 %fusion = bf16[6144,128]{0,1:T(8,128)(2,1)} fusion(bf16[6144,512]{1,0:T(8,128)(2,1)} %all-gather.5.cloned.1.call-done, bf16[6144,128]{0,1:T(8,128)(2,1)} %all-reduce.2.cloned.1.call-done), kind=kOutput, calls=%fused_computation.1 | convolution fusion | flops 1611464704 | bytes 9437184 | tf_op jit(solution)/shard_map/dot_general | solution.py:42
  425.8 0.0 reduce-scatter.2.cloned.1.call-update
  425.8 57.5 %reduce-scatter.2.cloned.1.call-done = bf16[768,128]{0,1:T(8,128)(2,1)} async-done(((bf16[6144,128]{0,1:T(8,128)(2,1)}), bf16[768,128]{0,1:T(8,128)(2,1)}) %reduce-scatter.2.cloned.1.call-update) | async-done | bytes 196624 | tf_op jit(solution)/shard_map/reduce_scatter | solution.py:43
  483.4 1.1 convert_subtract_fusion
  484.4 0.9 copy.9
  (2 shorter events, 0.0 us)
Async XLA Ops:
  6.5 133.3 %all-gather.3.cloned.1.call-start = ((), (), s32[]{:S(2)}) async-start(), calls=%async_computation.1 | async-start | bytes 3194880 | tf_op jit(solution)/shard_map/all_gather | solution.py:25
  7.3 254.1 %all-reduce.2.cloned.1.call-start = ((), (), s32[]{:S(2)}) async-start(), calls=%async_computation.2 | async-start | bytes 3145728 | tf_op jit(solution)/shard_map/psum | solution.py:35
  144.9 271.6 %all-gather.5.cloned.1.call-start = ((), (), s32[]{:S(2)}) async-start(), calls=%async_computation.3 | async-start | bytes 6389760 | tf_op jit(solution)/shard_map/all_gather | solution.py:37
  145.6 337.8 %reduce-scatter.2.cloned.1.call-start = ((), (), s32[]{:S(2)}) async-start(), calls=%async_computation.4 | async-start | bytes 1769472 | tf_op jit(solution)/shard_map/reduce_scatter | solution.py:43
Sparse Core Ops, SparseCore 0:
  11.9 127.9 all-gather.2
  145.0 116.3 all-reduce.1
  265.9 150.5 all-gather.4
  426.0 57.3 reduce-scatter.1
where the time goes:
time: 497 us; the launch traced here: 492 us
  waiting for transfers between devices  460 us (93%)
  between operations  13.2 us (3%)
  matrix products  12.5 us (3%)
    all_gather x1, waiting for transfers between devices, on_device(): panel_full = lax.all_gather(basis, 'fsdp', axis=0, tiled=True)  155 us
    all_gather x1, waiting for transfers between devices, on_device(): features = lax.all_gather(activations, 'fsdp', axis=1, tiled=True)  131 us
    psum x1, waiting for transfers between devices, on_device(): gradient = lax.psum(partial_value.astype(jnp.bfloat16), 'basis')  116 us
    reduce_scatter x1, waiting for transfers between devices, on_device(): lax.psum_scatter(removal_part.astype(jnp.bfloat16), 'basis', scatter_dime...  57.5 us
  transfers between devices with their start and end apart: 4, of which 4 were waited for; matrix products, arithmetic and copies ran while one was open for 0% of the time, Pallas kernels for 0%

commit v1 on v0

v1 whole, which is shorter than its diff:
```python
import jax
import jax.numpy as jnp
from jax import lax
from jax.sharding import Mesh, PartitionSpec as P

BLOCK = 128
SIZES = {"y": 4, "half": 2, "x": 4, "core": 2, "z": 8}


def routed(value, axes, target):
    sizes = [SIZES[a] for a in axes]
    pairs = []
    coords = [()]
    for s in sizes:
        coords = [c + (i,) for c in coords for i in range(s)]
    flat = {c: i for i, c in enumerate(coords)}
    for c in coords:
        pairs.append((flat[c], flat[tuple(target(*c))]))
    return lax.ppermute(value, axes, pairs)


def swap_z(value, bit):
    return routed(value, ("z",), lambda z: (z ^ bit,))


def swap_core(value):
    return routed(value, ("core",), lambda c: (1 - c,))


def ordered(flag, first, second, axis):
    return jnp.concatenate(
        [jnp.where(flag, second, first), jnp.where(flag, first, second)], axis=axis
    )


def masked_grad(hidden_grad, block_rows):
    tokens, width = hidden_grad.shape
    position = lax.broadcasted_iota(jnp.int32, (BLOCK, width), 0)
    parts = [
        jnp.where(
            position < block_rows[i], hidden_grad[i * BLOCK : (i + 1) * BLOCK], 0
        ).astype(hidden_grad.dtype)
        for i in range(tokens // BLOCK)
    ]
    return jnp.concatenate(parts, axis=0)


def on_device(activations, hidden_grad, block_rows, basis, accumulated):
    half, core, z = lax.axis_index("half"), lax.axis_index("core"), lax.axis_index("z")
    f32, bf16 = jnp.float32, jnp.bfloat16
    rows, width = accumulated.shape

    def basis_target(s):
        def target(y, h, z):
            m = z & 3
            return (
                (((y & 1) ^ (m >> 1)) << 1) | (h ^ (m & 1)),
                (z >> 2) ^ s,
                ((y >> 1) << 2) | m,
            )

        return target

    axes = ("y", "half", "z")
    b0 = routed(basis, axes, basis_target(0))
    b1 = routed(basis, axes, basis_target(1))
    strip = ordered(half == 1, b0, b1, 1)
    panel = lax.all_gather(strip, ("y", "x", "core"), axis=0, tiled=True)

    def act_target(s):
        return lambda y, h, z: ((z >> 1) ^ y, (z & 1) ^ s, 2 * y + h)

    act_t = activations.T
    a0 = routed(act_t, axes, act_target(0))
    a1 = routed(act_t, axes, act_target(1))
    act_strip = ordered((half ^ (z & 1)) == 1, a0, a1, 1)
    act_all = lax.all_to_all(
        jnp.broadcast_to(act_strip, (16,) + act_strip.shape), ("y", "x"), 0, 0
    )
    act_all = act_all.reshape(4, -1, act_strip.shape[1])

    grad = masked_grad(hidden_grad, block_rows)
    g = jnp.stack([grad, swap_z(grad, 4)], axis=0)
    g = jnp.stack([g, swap_z(g, 2)], axis=1)
    g = jnp.stack([g, swap_z(g, 1)], axis=2)
    g = g.reshape(4, -1, width)
    g_other = swap_core(g)

    def product(right):
        total = jnp.zeros((act_all.shape[1], width), f32)
        for i in range(4):
            total = total + jnp.dot(act_all[i], right[i], preferred_element_type=f32)
        return total.reshape(4, 1, -1, width)

    theirs = swap_core(product(g_other))
    mine = product(g)
    gradient = ordered(core == 1, mine, theirs, 1).reshape(rows, width) + accumulated
    gradient = gradient.astype(bf16)

    wide = jnp.stack([gradient, swap_z(gradient, 2)], axis=0)
    wide = jnp.stack([wide, swap_z(wide, 1)], axis=1).reshape(4 * rows, width)

    coeffs = lax.dot_general(
        panel, wide, (((0,), (0,)), ((), ())), preferred_element_type=f32
    )
    coeffs = (coeffs + swap_z(coeffs.astype(bf16), 4).astype(f32)).astype(bf16)
    removal = jnp.dot(panel, coeffs, preferred_element_type=f32)
    removal = removal.reshape(2, 2, rows, width)
    kept = removal[:, 0] + swap_z(removal[:, 1].astype(bf16), 1).astype(f32)
    removed = kept[0] + swap_z(kept[1].astype(bf16), 2).astype(f32)
    return gradient.astype(f32) - removed


def solution(mesh):
    grid = Mesh(mesh.devices.reshape(tuple(SIZES.values())), tuple(SIZES))
    fsdp = ("y", "half", "x", "core")
    placed = (P("z", fsdp), P("z", fsdp), P("z"), P(fsdp, "z"), P("z", fsdp))
    return jax.shard_map(
        on_device, mesh=grid, in_specs=placed, out_specs=P("z", fsdp), check_vma=False
    )
```

time: 497 us -> 203 us (0.41)
  waiting for transfers between devices: 460 us -> 95.2 us
  starting transfers between devices: 0.12 us -> 77.4 us
    all_gather x2 -> x1, waiting for transfers between devices: 286 us -> 0.02 us  [on_device(): panel = lax.all_gather(strip, ('y', 'x', 'core'), axis=0, tiled=True)]
    psum x1 -> x0, waiting for transfers between devices: 116 us -> none  [on_device(): gradient = lax.psum(partial_value.astype(jnp.bfloat16), 'basis')]
    ppermute x0 -> x14, waiting for transfers between devices: none -> 95.2 us  [routed(): return lax.ppermute(value, axes, pairs)]
    ppermute x0 -> x14, starting transfers between devices: none -> 62.3 us  [routed(): return lax.ppermute(value, axes, pairs)]
    reduce_scatter x1 -> x0, waiting for transfers between devices: 57.5 us -> none  [on_device(): lax.psum_scatter(removal_part.astype(jnp.bfloat16), 'basis', scatter_dime...]
    all_to_all x0 -> x1, starting transfers between devices: none -> 15.1 us  [on_device(): lax.all_to_all(jnp.broadcast_to(act_strip, (16,) + act_strip.shape), ('y'...]
    dot_general x2 -> x10, matrix products: 12.5 us -> 8.64 us  [the longest x1 4.75 us: on_device(): lax.dot_general(panel, wide, (((0,), (0,)), ((), ())), preferred_element_...]
  transfers between devices with their start and end apart: 4 -> 16, of which waited for: 4 -> 11; matrix products, arithmetic and copies ran while one was open for 0% -> 3% of each run, Pallas kernels for 0% -> 0%
where the time goes in v1:
time: 203 us; the launch traced here: 202 us
  waiting for transfers between devices  95.2 us (47%)
  starting transfers between devices  77.4 us (38%)
  between operations  13.7 us (7%)
  matrix products  8.64 us (4%)
  local copies, waits for them, and re-layouts  3.52 us (2%)
  other arithmetic  3.29 us (2%)
    ppermute x14, waiting for transfers between devices, routed(): return lax.ppermute(value, axes, pairs)  95.2 us
    ppermute x14, starting transfers between devices, routed(): return lax.ppermute(value, axes, pairs)  62.3 us
    all_to_all x1, starting transfers between devices, on_device(): lax.all_to_all(jnp.broadcast_to(act_strip, (16,) + act_strip.shape), ('y'...  15.1 us
    dot_general x1, matrix products, on_device(): lax.dot_general(panel, wide, (((0,), (0,)), ((), ())), preferred_element_...  4.75 us
  transfers between devices with their start and end apart: 16, of which 11 were waited for; matrix products, arithmetic and copies ran while one was open for 3% of the time, Pallas kernels for 0%

profile of v1, /device:TPU:1, one launch (start us, length us, event | category | flops | bytes accessed | tf_op | source)
XLA Modules:
  0.0 201.8 jit_solution(12247736347069999440)
XLA Ops:
  6.5 0.0 all-gather.2.cloned.1.call-start
  6.5 16.3 %collective-permute-start.7 = (bf16[96,512]{1,0:T(8,128)(2,1)}, bf16[96,512]{1,0:T(8,128)(2,1)S(1)}, u32[]{:S(2)}, u32[]{:S(2)}) collective-permute-start(bf16[96,512]{1,0:T(8,128)(2,1)} %param.8), channel_id=1, source_target_pairs={{0,64},{1,193},{2,322},{3,451},{4,0},{5,129},{6,258},{7,387},{64,1... | collective-permute-start | bytes 294920 | tf_op jit(solution)/shard_map/ppermute | solution.py:19
  22.8 1.6 collective-permute-start.8
  24.4 5.2 %collective-permute-done.7 = bf16[96,512]{1,0:T(8,128)(2,1)S(1)} collective-permute-done((bf16[96,512]{1,0:T(8,128)(2,1)}, bf16[96,512]{1,0:T(8,128)(2,1)S(1)}, u32[]{:S(2)}, u32[]{:S(2)}) %collective-permute-start.7) | collective-permute-done | bytes 98336 | tf_op jit(solution)/shard_map/ppermute | solution.py:19
  29.6 0.0 collective-permute-done.8
  29.6 0.7 pad_maximum_fusion.5
  30.3 0.0 all-gather.2.cloned.1.call-update
  30.3 12.7 %collective-permute-start = (bf16[96,256]{1,0:T(8,128)(2,1)}, bf16[96,256]{1,0:T(8,128)(2,1)S(1)}, u32[]{:S(2)}, u32[]{:S(2)}) collective-permute-start(bf16[96,256]{1,0:T(8,128)(2,1)} %bitcast.109), channel_id=1, source_target_pairs={{0,64},{1,0},{2,192},{3,128},{4,320},{5,256},{6,448},{7,384},{64,6... | collective-permute-start | bytes 147464 | tf_op jit(solution)/shard_map/ppermute | solution.py:19
  43.1 1.5 collective-permute-start.1
  44.5 1.3 fusion.18
  45.8 0.5 collective-permute-done
  46.4 0.0 collective-permute-done.1
  46.4 1.3 broadcast_in_dim.8
  47.7 0.0 copy-start.2
  47.7 15.1 %all-to-all-start = ((bf16[16,96,512]{2,1,0:T(8,128)(2,1)}), bf16[16,96,512]{2,1,0:T(8,128)(2,1)S(1)}, u32[]{:S(2)}, u32[]{:S(2)}) async-start(bf16[16,96,512]{2,1,0:T(8,128)(2,1)} %broadcast_in_dim.8), calls=%async_computation | async-start | bytes 3145728 | tf_op jit(solution)/shard_map/all_to_all | solution.py:77
  62.8 1.2 iota_compare_fusion
  64.0 0.0 copy-done.2
  64.0 0.1 slice_select_fusion.1
  64.1 2.7 %collective-permute-start.2 = (bf16[256,128]{1,0:T(8,128)(2,1)S(1)}, bf16[256,128]{1,0:T(8,128)(2,1)S(1)}, u32[]{:S(2)}, u32[]{:S(2)}) collective-permute-start(bf16[256,128]{1,0:T(8,128)(2,1)S(1)} %get-tuple-element.22), channel_id=1, source_target_pairs={{0,4},{1,5},{2,6},{3,7},{4,0},{5,1},{6,2},{7,3},{8,12},{9,13},{10,... | collective-permute-start | bytes 196616 | tf_op jit(solution)/shard_map/ppermute | solution.py:19
  66.8 6.9 %collective-permute-done.2 = bf16[256,128]{1,0:T(8,128)(2,1)S(1)} collective-permute-done((bf16[256,128]{1,0:T(8,128)(2,1)S(1)}, bf16[256,128]{1,0:T(8,128)(2,1)S(1)}, u32[]{:S(2)}, u32[]{:S(2)}) %collective-permute-start.2) | collective-permute-done | bytes 65568 | tf_op jit(solution)/shard_map/ppermute | solution.py:19
  73.7 2.1 %collective-permute-start.3 = (bf16[2,256,128]{2,1,0:T(8,128)(2,1)S(1)}, bf16[2,256,128]{2,1,0:T(8,128)(2,1)S(1)}, u32[]{:S(2)}, u32[]{:S(2)}) collective-permute-start(bf16[2,256,128]{2,1,0:T(8,128)(2,1)S(1)} %get-tuple-element.18), channel_id=1, source_target_pairs={{0,2},{1,3},{2,0},{3,1},{4,6},{5,7},{6,4},{7,5},{8,10},{9,11},{10,... | collective-permute-start | bytes 393224 | tf_op jit(solution)/shard_map/ppermute | solution.py:19
  75.8 6.9 %collective-permute-done.3 = bf16[2,256,128]{2,1,0:T(8,128)(2,1)S(1)} collective-permute-done((bf16[2,256,128]{2,1,0:T(8,128)(2,1)S(1)}, bf16[2,256,128]{2,1,0:T(8,128)(2,1)S(1)}, u32[]{:S(2)}, u32[]{:S(2)}) %collective-permute-start.3) | collective-permute-done | bytes 131104 | tf_op jit(solution)/shard_map/ppermute | solution.py:19
  82.8 1.9 collective-permute-start.4
  84.7 6.6 %collective-permute-done.4 = bf16[2,2,256,128]{3,2,1,0:T(8,128)(2,1)S(1)} collective-permute-done((bf16[2,2,256,128]{3,2,1,0:T(8,128)(2,1)S(1)}, bf16[2,2,256,128]{3,2,1,0:T(8,128)(2,1)S(1)}, u32[]{:S(2)}, u32[]{:S(2)}) %collective-permute-start.4) | collective-permute-done | bytes 262176 | tf_op jit(solution)/shard_map/ppermute | solution.py:19
  91.3 0.1 pad_maximum_fusion.1
  91.4 8.5 %collective-permute-start.5 = (bf16[4,512,128]{2,1,0:T(8,128)(2,1)S(1)}, bf16[4,512,128]{2,1,0:T(8,128)(2,1)S(1)}, u32[]{:S(2)}, u32[]{:S(2)}) collective-permute-start(bf16[4,512,128]{2,1,0:T(8,128)(2,1)S(1)} %bitcast.96), channel_id=1, source_target_pairs={{0,8},{8,0},{1,9},{9,1},{2,10},{10,2},{3,11},{11,3},{4,12},{12,4},... | collective-permute-start | bytes 1572872 | tf_op jit(solution)/shard_map/ppermute | solution.py:19
  99.9 0.0 all-to-all-done
  99.9 0.1 fusion.17
  100.0 1.4 collective-permute-done.5
  101.4 0.3 fusion.12
  101.7 0.3 fusion.11
  101.9 0.3 fusion.10
  102.2 0.3 fusion.1
  102.5 2.3 %collective-permute-start.6 = (f32[4,1,96,128]{3,2,0,1:T(8,128)S(1)}, f32[4,1,96,128]{3,2,0,1:T(8,128)S(1)}, u32[]{:S(2)}, u32[]{:S(2)}) collective-permute-start(f32[4,1,96,128]{3,2,0,1:T(8,128)S(1)} %bitcast.105), channel_id=1, source_target_pairs={{0,8},{8,0},{1,9},{9,1},{2,10},{10,2},{3,11},{11,3},{4,12},{12,4},... | collective-permute-start | bytes 589832 | tf_op jit(solution)/shard_map/ppermute | solution.py:19
  104.7 0.3 fusion.9
  105.0 0.3 convolution_add_fusion.2
  105.3 0.3 convolution_add_fusion.1
  105.5 0.0 copy-start.1
  105.6 0.3 convolution_add_fusion
  105.8 0.0 collective-permute-done.6
  105.9 0.7 copy-done.1
  106.6 0.1 fusion.6
  106.7 4.5 %collective-permute-start.9 = (bf16[768,128]{1,0:T(8,128)(2,1)S(1)}, bf16[768,128]{1,0:T(8,128)(2,1)S(1)}, u32[]{:S(2)}, u32[]{:S(2)}) collective-permute-start(bf16[768,128]{1,0:T(8,128)(2,1)S(1)} %fusion.6), channel_id=1, source_target_pairs={{0,2},{1,3},{2,0},{3,1},{4,6},{5,7},{6,4},{7,5},{8,10},{9,11},{10,... | collective-permute-start | bytes 589832 | tf_op jit(solution)/shard_map/ppermute | solution.py:19
  111.2 9.3 %collective-permute-done.9 = bf16[768,128]{1,0:T(8,128)(2,1)S(1)} collective-permute-done((bf16[768,128]{1,0:T(8,128)(2,1)S(1)}, bf16[768,128]{1,0:T(8,128)(2,1)S(1)}, u32[]{:S(2)}, u32[]{:S(2)}) %collective-permute-start.9) | collective-permute-done | bytes 196640 | tf_op jit(solution)/shard_map/ppermute | solution.py:19
  120.5 0.1 fusion.16
  120.5 2.6 %collective-permute-start.10 = (bf16[2,768,128]{2,1,0:T(8,128)(2,1)S(1)}, bf16[2,768,128]{2,1,0:T(8,128)(2,1)S(1)}, u32[]{:S(2)}, u32[]{:S(2)}) collective-permute-start(bf16[2,768,128]{2,1,0:T(8,128)(2,1)S(1)} %get-tuple-element.10), channel_id=1, source_target_pairs={{0,1},{1,0},{2,3},{3,2},{4,5},{5,4},{6,7},{7,6},{8,9},{9,8},{10,11... | collective-permute-start | bytes 1179656 | tf_op jit(solution)/shard_map/ppermute | solution.py:19
  123.2 9.2 %collective-permute-done.10 = bf16[2,768,128]{2,1,0:T(8,128)(2,1)S(1)} collective-permute-done((bf16[2,768,128]{2,1,0:T(8,128)(2,1)S(1)}, bf16[2,768,128]{2,1,0:T(8,128)(2,1)S(1)}, u32[]{:S(2)}, u32[]{:S(2)}) %collective-permute-start.10) | collective-permute-done | bytes 393248 | tf_op jit(solution)/shard_map/ppermute | solution.py:19
  132.4 0.1 pad_maximum_fusion
  132.4 0.0 all-gather.2.cloned.1.call-done
  132.5 0.0 copy-start
  132.5 4.8 %fusion.19 = (bf16[1024,128]{1,0:T(8,128)(2,1)S(1)}, f32[1024,128]{1,0:T(8,128)S(1)}) fusion(bf16[3072,1024]{1,0:T(8,128)(2,1)} %all-gather.2.cloned.1.call-done, bf16[3072,128]{1,0:T(8,128)(2,1)S(1)} %bitcast.95), kind=kOutput, calls=%fused_computation.56 | convolution fusion | flops 805437440 | bytes 7864320 | tf_op jit(solution)/shard_map/dot_general | solution.py:103
  137.2 1.9 collective-permute-start.11
  139.2 28.2 %collective-permute-done.11 = bf16[1024,128]{1,0:T(8,128)(2,1)S(1)} collective-permute-done((bf16[1024,128]{1,0:T(8,128)(2,1)S(1)}, bf16[1024,128]{1,0:T(8,128)(2,1)S(1)}, u32[]{:S(2)}, u32[]{:S(2)}) %collective-permute-start.11) | collective-permute-done | bytes 262176 | tf_op jit(solution)/shard_map/ppermute | solution.py:19
  167.3 0.0 copy-done
  167.3 1.8 fusion.7
  169.1 0.1 fusion.3
  169.2 1.9 collective-permute-start.12
  171.1 9.3 %collective-permute-done.12 = bf16[2,768,128]{2,1,0:T(8,128)(2,1)S(1)} collective-permute-done((bf16[2,768,128]{2,1,0:T(8,128)(2,1)S(1)}, bf16[2,768,128]{2,1,0:T(8,128)(2,1)S(1)}, u32[]{:S(2)}, u32[]{:S(2)}) %collective-permute-start.12) | collective-permute-done | bytes 393248 | tf_op jit(solution)/shard_map/ppermute | solution.py:19
  180.4 0.1 fusion.2
  180.5 1.9 collective-permute-start.13
  182.5 11.7 %collective-permute-done.13 = bf16[768,128]{1,0:T(8,128)(2,1)S(1)} collective-permute-done((bf16[768,128]{1,0:T(8,128)(2,1)S(1)}, bf16[768,128]{1,0:T(8,128)(2,1)S(1)}, u32[]{:S(2)}, u32[]{:S(2)}) %collective-permute-start.13) | collective-permute-done | bytes 196640 | tf_op jit(solution)/shard_map/ppermute | solution.py:19
  194.2 0.8 fusion.5
  (10 shorter events, 0.2 us)
Async XLA Ops:
  6.5 125.9 %all-gather.2.cloned.1.call-start = ((), (), s32[]{:S(2)}) async-start(), calls=%async_computation.1 | async-start | bytes 6488064 | tf_op jit(solution)/shard_map/all_gather | solution.py:68
  6.5 23.1 %collective-permute-start.7 = (bf16[96,512]{1,0:T(8,128)(2,1)}, bf16[96,512]{1,0:T(8,128)(2,1)S(1)}, u32[]{:S(2)}, u32[]{:S(2)}) collective-permute-start(bf16[96,512]{1,0:T(8,128)(2,1)} %param.8), channel_id=1, source_target_pairs={{0,64},{1,193},{2,322},{3,451},{4,0},{5,129},{6,258},{7,387},{64,1... | collective-permute-start | bytes 294920 | tf_op jit(solution)/shard_map/ppermute | solution.py:19
  22.8 6.8 %collective-permute-start.8 = (bf16[96,512]{1,0:T(8,128)(2,1)}, bf16[96,512]{1,0:T(8,128)(2,1)S(1)}, u32[]{:S(2)}, u32[]{:S(2)}) collective-permute-start(bf16[96,512]{1,0:T(8,128)(2,1)} %param.8), channel_id=1, source_target_pairs={{0,0},{1,129},{2,258},{3,387},{4,64},{5,193},{6,322},{7,451},{64,1... | collective-permute-start | bytes 294920 | tf_op jit(solution)/shard_map/ppermute | solution.py:19
  30.3 16.0 %collective-permute-start = (bf16[96,256]{1,0:T(8,128)(2,1)}, bf16[96,256]{1,0:T(8,128)(2,1)S(1)}, u32[]{:S(2)}, u32[]{:S(2)}) collective-permute-start(bf16[96,256]{1,0:T(8,128)(2,1)} %bitcast.109), channel_id=1, source_target_pairs={{0,64},{1,0},{2,192},{3,128},{4,320},{5,256},{6,448},{7,384},{64,6... | collective-permute-start | bytes 147464 | tf_op jit(solution)/shard_map/ppermute | solution.py:19
  43.1 3.3 %collective-permute-start.1 = (bf16[96,256]{1,0:T(8,128)(2,1)}, bf16[96,256]{1,0:T(8,128)(2,1)S(1)}, u32[]{:S(2)}, u32[]{:S(2)}) collective-permute-start(bf16[96,256]{1,0:T(8,128)(2,1)} %bitcast.110), channel_id=1, source_target_pairs={{0,0},{1,64},{2,128},{3,192},{4,256},{5,320},{6,384},{7,448},{64,1... | collective-permute-start | bytes 147464 | tf_op jit(solution)/shard_map/ppermute | solution.py:19
  47.7 16.3 %copy-start.2 = (bf16[256,128]{1,0:T(8,128)(2,1)S(1)}, bf16[256,128]{1,0:T(8,128)(2,1)}, u32[]{:S(2)}) copy-start(bf16[256,128]{1,0:T(8,128)(2,1)} %param.6) | copy-start | bytes 196612
  47.7 52.2 %all-to-all-start = ((bf16[16,96,512]{2,1,0:T(8,128)(2,1)}), bf16[16,96,512]{2,1,0:T(8,128)(2,1)S(1)}, u32[]{:S(2)}, u32[]{:S(2)}) async-start(bf16[16,96,512]{2,1,0:T(8,128)(2,1)} %broadcast_in_dim.8), calls=%async_computation | async-start | bytes 3145728 | tf_op jit(solution)/shard_map/all_to_all | solution.py:77
  64.1 9.6 %collective-permute-start.2 = (bf16[256,128]{1,0:T(8,128)(2,1)S(1)}, bf16[256,128]{1,0:T(8,128)(2,1)S(1)}, u32[]{:S(2)}, u32[]{:S(2)}) collective-permute-start(bf16[256,128]{1,0:T(8,128)(2,1)S(1)} %get-tuple-element.22), channel_id=1, source_target_pairs={{0,4},{1,5},{2,6},{3,7},{4,0},{5,1},{6,2},{7,3},{8,12},{9,13},{10,... | collective-permute-start | bytes 196616 | tf_op jit(solution)/shard_map/ppermute | solution.py:19
  73.7 9.0 %collective-permute-start.3 = (bf16[2,256,128]{2,1,0:T(8,128)(2,1)S(1)}, bf16[2,256,128]{2,1,0:T(8,128)(2,1)S(1)}, u32[]{:S(2)}, u32[]{:S(2)}) collective-permute-start(bf16[2,256,128]{2,1,0:T(8,128)(2,1)S(1)} %get-tuple-element.18), channel_id=1, source_target_pairs={{0,2},{1,3},{2,0},{3,1},{4,6},{5,7},{6,4},{7,5},{8,10},{9,11},{10,... | collective-permute-start | bytes 393224 | tf_op jit(solution)/shard_map/ppermute | solution.py:19
  82.8 8.5 %collective-permute-start.4 = (bf16[2,2,256,128]{3,2,1,0:T(8,128)(2,1)S(1)}, bf16[2,2,256,128]{3,2,1,0:T(8,128)(2,1)S(1)}, u32[]{:S(2)}, u32[]{:S(2)}) collective-permute-start(bf16[2,2,256,128]{3,2,1,0:T(8,128)(2,1)S(1)} %get-tuple-element.14), channel_id=1, source_target_pairs={{0,1},{1,0},{2,3},{3,2},{4,5},{5,4},{6,7},{7,6},{8,9},{9,8},{10,11... | collective-permute-start | bytes 786440 | tf_op jit(solution)/shard_map/ppermute | solution.py:19
  91.4 10.0 %collective-permute-start.5 = (bf16[4,512,128]{2,1,0:T(8,128)(2,1)S(1)}, bf16[4,512,128]{2,1,0:T(8,128)(2,1)S(1)}, u32[]{:S(2)}, u32[]{:S(2)}) collective-permute-start(bf16[4,512,128]{2,1,0:T(8,128)(2,1)S(1)} %bitcast.96), channel_id=1, source_target_pairs={{0,8},{8,0},{1,9},{9,1},{2,10},{10,2},{3,11},{11,3},{4,12},{12,4},... | collective-permute-start | bytes 1572872 | tf_op jit(solution)/shard_map/ppermute | solution.py:19
  102.5 3.4 %collective-permute-start.6 = (f32[4,1,96,128]{3,2,0,1:T(8,128)S(1)}, f32[4,1,96,128]{3,2,0,1:T(8,128)S(1)}, u32[]{:S(2)}, u32[]{:S(2)}) collective-permute-start(f32[4,1,96,128]{3,2,0,1:T(8,128)S(1)} %bitcast.105), channel_id=1, source_target_pairs={{0,8},{8,0},{1,9},{9,1},{2,10},{10,2},{3,11},{11,3},{4,12},{12,4},... | collective-permute-start | bytes 589832 | tf_op jit(solution)/shard_map/ppermute | solution.py:19
  105.5 1.1 copy-start.1
  106.7 13.8 %collective-permute-start.9 = (bf16[768,128]{1,0:T(8,128)(2,1)S(1)}, bf16[768,128]{1,0:T(8,128)(2,1)S(1)}, u32[]{:S(2)}, u32[]{:S(2)}) collective-permute-start(bf16[768,128]{1,0:T(8,128)(2,1)S(1)} %fusion.6), channel_id=1, source_target_pairs={{0,2},{1,3},{2,0},{3,1},{4,6},{5,7},{6,4},{7,5},{8,10},{9,11},{10,... | collective-permute-start | bytes 589832 | tf_op jit(solution)/shard_map/ppermute | solution.py:19
  120.5 11.8 %collective-permute-start.10 = (bf16[2,768,128]{2,1,0:T(8,128)(2,1)S(1)}, bf16[2,768,128]{2,1,0:T(8,128)(2,1)S(1)}, u32[]{:S(2)}, u32[]{:S(2)}) collective-permute-start(bf16[2,768,128]{2,1,0:T(8,128)(2,1)S(1)} %get-tuple-element.10), channel_id=1, source_target_pairs={{0,1},{1,0},{2,3},{3,2},{4,5},{5,4},{6,7},{7,6},{8,9},{9,8},{10,11... | collective-permute-start | bytes 1179656 | tf_op jit(solution)/shard_map/ppermute | solution.py:19
  132.5 34.9 %copy-start = (bf16[3072,1024]{1,0:T(8,128)(2,1)S(1)}, bf16[3072,1024]{1,0:T(8,128)(2,1)}, u32[]{:S(2)}) copy-start(bf16[3072,1024]{1,0:T(8,128)(2,1)} %all-gather.2.cloned.1.call-done) | copy-start | bytes 18874372
  137.2 30.1 %collective-permute-start.11 = (bf16[1024,128]{1,0:T(8,128)(2,1)S(1)}, bf16[1024,128]{1,0:T(8,128)(2,1)S(1)}, u32[]{:S(2)}, u32[]{:S(2)}) collective-permute-start(bf16[1024,128]{1,0:T(8,128)(2,1)S(1)} %get-tuple-element.27), channel_id=1, source_target_pairs={{0,4},{1,5},{2,6},{3,7},{4,0},{5,1},{6,2},{7,3},{8,12},{9,13},{10,... | collective-permute-start | bytes 786440 | tf_op jit(solution)/shard_map/ppermute | solution.py:19
  169.2 11.2 %collective-permute-start.12 = (bf16[2,768,128]{2,1,0:T(8,128)(2,1)S(1)}, bf16[2,768,128]{2,1,0:T(8,128)(2,1)S(1)}, u32[]{:S(2)}, u32[]{:S(2)}) collective-permute-start(bf16[2,768,128]{2,1,0:T(8,128)(2,1)S(1)} %fusion.3), channel_id=1, source_target_pairs={{0,1},{1,0},{2,3},{3,2},{4,5},{5,4},{6,7},{7,6},{8,9},{9,8},{10,11... | collective-permute-start | bytes 1179656 | tf_op jit(solution)/shard_map/ppermute | solution.py:19
  180.5 13.6 %collective-permute-start.13 = (bf16[768,128]{1,0:T(8,128)(2,1)S(1)}, bf16[768,128]{1,0:T(8,128)(2,1)S(1)}, u32[]{:S(2)}, u32[]{:S(2)}) collective-permute-start(bf16[768,128]{1,0:T(8,128)(2,1)S(1)} %fusion.8), channel_id=1, source_target_pairs={{0,2},{1,3},{2,0},{3,1},{4,6},{5,7},{6,4},{7,5},{8,10},{9,11},{10,... | collective-permute-start | bytes 589832 | tf_op jit(solution)/shard_map/ppermute | solution.py:19
Sparse Core Ops, SparseCore 0:
  30.5 84.8 all-gather.1

commit v2 on v1

v2 whole, which is shorter than its diff:
```python
import jax
import jax.numpy as jnp
from jax import lax
from jax.sharding import Mesh, PartitionSpec as P

BLOCK = 128
SIZES = {"y": 4, "half": 2, "x": 4, "core": 2, "z": 8}
PAIR, FAR, NEAR = 1, 2, 0
ROUTE = ("y", "half", "z")


def bit(value, i):
    return (value >> i) & 1


def routed(value, axes, target):
    coords = [()]
    for a in axes:
        coords = [c + (i,) for c in coords for i in range(SIZES[a])]
    flat = {c: i for i, c in enumerate(coords)}
    return lax.ppermute(value, axes, [(flat[c], flat[tuple(target(*c))]) for c in coords])


def swap_z(value, i):
    return routed(value, ("z",), lambda z: (z ^ (1 << i),))


def swap_core(value):
    return routed(value, ("core",), lambda c: (1 - c,))


def basis_target(s):
    def target(y, h, z):
        b = 2 * y + h
        plane = (z & ~(1 << PAIR)) | (bit(b, PAIR) << PAIR)
        slot = b ^ plane
        return 2 * bit(slot, FAR) + bit(slot, NEAR), bit(z, PAIR) ^ s, plane

    return target


def act_target(s):
    return lambda y, h, z: ((z >> 1) ^ y, (z & 1) ^ s, 2 * y + h)


def ordered(flag, first, second, axis):
    return jnp.concatenate(
        [jnp.where(flag, second, first), jnp.where(flag, first, second)], axis=axis
    )


def masked_grad(hidden_grad, block_rows):
    tokens, width = hidden_grad.shape
    position = lax.broadcasted_iota(jnp.int32, (BLOCK, width), 0)
    parts = [
        jnp.where(
            position < block_rows[i], hidden_grad[i * BLOCK : (i + 1) * BLOCK], 0
        ).astype(hidden_grad.dtype)
        for i in range(tokens // BLOCK)
    ]
    return jnp.concatenate(parts, axis=0)


def spread(strip):
    copies = jnp.broadcast_to(strip, (16,) + strip.shape)
    return lax.all_to_all(copies, ("y", "x"), 0, 0)


def on_device(activations, hidden_grad, block_rows, basis, accumulated):
    half, core, z = lax.axis_index("half"), lax.axis_index("core"), lax.axis_index("z")
    f32, bf16 = jnp.float32, jnp.bfloat16
    rows, width = accumulated.shape
    fence = lax.optimization_barrier

    act_t = activations.T
    a0, a1 = (routed(act_t, ROUTE, act_target(s)) for s in (0, 1))
    grad = masked_grad(hidden_grad, block_rows)
    g4 = swap_z(grad, 2)
    b0, b1 = (routed(basis, ROUTE, basis_target(s)) for s in (0, 1))

    act_strip = ordered((half ^ (z & 1)) == 1, a0, a1, 1)
    act_strip, grad, g4 = fence((act_strip, grad, g4))
    act_all = spread(act_strip).reshape(4, -1, act_strip.shape[1])
    g = jnp.stack([grad, g4], axis=0)
    g = jnp.stack([g, swap_z(g, 1)], axis=1)
    g = jnp.stack([g, swap_z(g, 0)], axis=2)
    g = g.reshape(4, -1, width)

    strip = ordered(half == 1, b0, b1, 1)
    act_all, strip, g = fence((act_all, strip, g))
    g_other = swap_core(g)
    panel = spread(strip).reshape(-1, strip.shape[1])

    def product(right):
        total = jnp.zeros((act_all.shape[1], width), f32)
        for i in range(4):
            total = total + jnp.dot(act_all[i], right[i], preferred_element_type=f32)
        return total

    theirs = swap_core(product(g_other))
    mine = product(g)
    split = accumulated.reshape(4, 2, -1, width)
    added = ordered(core == 1, split[:, 0], split[:, 1], 0).reshape(2, -1, width)
    gradient = (jnp.stack([mine, theirs]) + added).astype(bf16)

    wide = jnp.stack([gradient, swap_z(gradient, FAR)], axis=1)
    wide, panel = fence((wide, panel))
    panel_other = swap_core(panel)
    wide = jnp.stack([wide, swap_z(wide, NEAR)], axis=2)
    wide = wide.reshape(2, -1, width)

    def project(left, right):
        return lax.dot_general(
            left, right, (((0,), (0,)), ((), ())), preferred_element_type=f32
        )

    coeffs = project(panel, wide[0]) + project(panel_other, wide[1])
    coeffs = (coeffs + swap_z(coeffs.astype(bf16), PAIR).astype(f32)).astype(bf16)
    removal = jnp.stack(
        [
            jnp.dot(p, coeffs, preferred_element_type=f32).reshape(2, 2, -1, width)
            for p in (panel, panel_other)
        ]
    )
    kept = removal[:, :, 0] + swap_z(removal[:, :, 1].astype(bf16), NEAR).astype(f32)
    removed = kept[:, 0] + swap_z(kept[:, 1].astype(bf16), FAR).astype(f32)
    result = (gradient.astype(f32) - removed).reshape(2, 4, 1, -1, width)
    return ordered(core == 1, result[0], result[1], 1).reshape(rows, width)


def solution(mesh):
    grid = Mesh(mesh.devices.reshape(tuple(SIZES.values())), tuple(SIZES))
    fsdp = ("y", "half", "x", "core")
    placed = (P("z", fsdp), P("z", fsdp), P("z"), P(fsdp, "z"), P("z", fsdp))
    return jax.shard_map(
        on_device, mesh=grid, in_specs=placed, out_specs=P("z", fsdp), check_vma=False
    )
```

time: 203 us -> 203 us (level)
  between operations: 13.7 us -> 0.5 us
  starting transfers between devices: 77.4 us -> 83 us
  waiting for transfers between devices: 95.2 us -> 99.4 us
  other arithmetic: 3.29 us -> 6.67 us
  local copies, waits for them, and re-layouts: 3.52 us -> 5.78 us
    ppermute x14 -> x15, starting transfers between devices: 62.3 us -> 73.2 us  [routed(): lax.ppermute(value, axes, [(flat[c], flat[tuple(target(*c))]) for c in co...]
    all_to_all x1 -> x2, waiting for transfers between devices: 0.01 us -> 6.89 us  [spread(): return lax.all_to_all(copies, ('y', 'x'), 0, 0)]
    all_to_all x1 -> x2, starting transfers between devices: 15.1 us -> 9.78 us  [spread(): return lax.all_to_all(copies, ('y', 'x'), 0, 0)]
    ppermute x14 -> x15, waiting for transfers between devices: 95.2 us -> 92.5 us  [routed(): lax.ppermute(value, axes, [(flat[c], flat[tuple(target(*c))]) for c in co...]
    another operation x6, other arithmetic: 0.24 us -> 2.89 us  [the longest x1 1.09 us: on_device(): wide = jnp.stack([wide, swap_z(wide, NEAR)], axis=2)]
    dot_general x2 -> x4, matrix products: 6.56 us -> 3.98 us  [the longest x2 2.02 us: project(): lax.dot_general(left, right, (((0,), (0,)), ((), ())), preferred_element_...]
    broadcast_in_dim x1 -> x2, local copies, waits for them, and re-layouts: 1.29 us -> 3.46 us  [spread(): copies = jnp.broadcast_to(strip, (16,) + strip.shape)]
  transfers between devices with their start and end apart: 16 -> 17, of which waited for: 11 -> 10; matrix products, arithmetic and copies ran while one was open for 3% -> 6% of each run, Pallas kernels for 0% -> 0%
where the time goes in v2:
time: 203 us; the launch traced here: 202 us
  waiting for transfers between devices  99.4 us (49%)
  starting transfers between devices  83 us (41%)
  matrix products  6.95 us (3%)
  other arithmetic  6.67 us (3%)
  local copies, waits for them, and re-layouts  5.78 us (3%)
    ppermute x15, waiting for transfers between devices, routed(): lax.ppermute(value, axes, [(flat[c], flat[tuple(target(*c))]) for c in co...  92.5 us
    ppermute x15, starting transfers between devices, routed(): lax.ppermute(value, axes, [(flat[c], flat[tuple(target(*c))]) for c in co...  73.2 us
    all_to_all x2, starting transfers between devices, spread(): return lax.all_to_all(copies, ('y', 'x'), 0, 0)  9.78 us
    all_to_all x2, waiting for transfers between devices, spread(): return lax.all_to_all(copies, ('y', 'x'), 0, 0)  6.89 us
  transfers between devices with their start and end apart: 17, of which 10 were waited for; matrix products, arithmetic and copies ran while one was open for 6% of the time, Pallas kernels for 0%

profile of v2, /device:TPU:1, one launch (start us, length us, event | category | flops | bytes accessed | tf_op | source)
XLA Modules:
  0.0 202.3 jit_solution(14390190616842558924)
XLA Ops:
  0.0 1.4 collective-permute-start.1
  1.4 16.7 %collective-permute-start = (bf16[96,256]{1,0:T(8,128)(2,1)}, bf16[96,256]{1,0:T(8,128)(2,1)S(1)}, u32[]{:S(2)}, u32[]{:S(2)}) collective-permute-start(bf16[96,256]{1,0:T(8,128)(2,1)} %bitcast.160), channel_id=1, source_target_pairs={{0,64},{1,0},{2,192},{3,128},{4,320},{5,256},{6,448},{7,384},{64,6... | collective-permute-start | bytes 147464 | tf_op jit(solution)/shard_map/ppermute | solution.py:21
  18.2 1.4 fusion.42
  19.6 1.3 iota_compare_fusion
  20.9 0.9 slice_select_fusion.3
  21.8 4.8 %collective-permute-start.2 = (bf16[256,128]{1,0:T(8,128)(2,1)S(1)}, bf16[256,128]{1,0:T(8,128)(2,1)S(1)}, u32[]{:S(2)}, u32[]{:S(2)}) collective-permute-start(bf16[256,128]{1,0:T(8,128)(2,1)S(1)} %pad_maximum_fusion.10), channel_id=1, source_target_pairs={{0,4},{1,5},{2,6},{3,7},{4,0},{5,1},{6,2},{7,3},{8,12},{9,13},{10,... | collective-permute-start | bytes 196616 | tf_op jit(solution)/shard_map/ppermute | solution.py:21
  26.6 0.0 collective-permute-done.1
  26.7 0.0 collective-permute-done
  26.7 9.6 %collective-permute-done.2 = bf16[256,128]{1,0:T(8,128)(2,1)S(1)} collective-permute-done((bf16[256,128]{1,0:T(8,128)(2,1)S(1)}, bf16[256,128]{1,0:T(8,128)(2,1)S(1)}, u32[]{:S(2)}, u32[]{:S(2)}) %collective-permute-start.2) | collective-permute-done | bytes 65568 | tf_op jit(solution)/shard_map/ppermute | solution.py:21
  36.3 1.3 broadcast_in_dim.12
  37.6 4.3 %all-to-all-start = ((bf16[16,96,512]{2,1,0:T(8,128)(2,1)}), bf16[16,96,512]{2,1,0:T(8,128)(2,1)S(1)}, u32[]{:S(2)}, u32[]{:S(2)}) async-start(bf16[16,96,512]{2,1,0:T(8,128)(2,1)} %broadcast_in_dim.12), calls=%async_computation | async-start | bytes 3145728 | tf_op jit(solution)/shard_map/all_to_all | solution.py:66
  41.9 2.8 %collective-permute-start.5 = (bf16[2,256,128]{2,1,0:T(8,128)(2,1)S(1)}, bf16[2,256,128]{2,1,0:T(8,128)(2,1)S(1)}, u32[]{:S(2)}, u32[]{:S(2)}) collective-permute-start(bf16[2,256,128]{2,1,0:T(8,128)(2,1)S(1)} %get-tuple-element.32), channel_id=1, source_target_pairs={{0,2},{1,3},{2,0},{3,1},{4,6},{5,7},{6,4},{7,5},{8,10},{9,11},{10,... | collective-permute-start | bytes 393224 | tf_op jit(solution)/shard_map/ppermute | solution.py:21
  44.7 0.0 copy-done.7
  44.7 0.7 collective-permute-start.4
  45.4 14.4 %collective-permute-start.3 = (bf16[96,512]{1,0:T(8,128)(2,1)S(1)}, bf16[96,512]{1,0:T(8,128)(2,1)S(1)}, u32[]{:S(2)}, u32[]{:S(2)}) collective-permute-start(bf16[96,512]{1,0:T(8,128)(2,1)S(1)} %copy-done.7), channel_id=1, source_target_pairs={{0,64},{1,193},{2,0},{3,129},{4,324},{5,453},{6,260},{7,389},{64,1... | collective-permute-start | bytes 294920 | tf_op jit(solution)/shard_map/ppermute | solution.py:21
  59.8 0.0 collective-permute-done.5
  59.9 2.1 %collective-permute-start.6 = (bf16[2,2,256,128]{3,2,1,0:T(8,128)(2,1)S(1)}, bf16[2,2,256,128]{3,2,1,0:T(8,128)(2,1)S(1)}, u32[]{:S(2)}, u32[]{:S(2)}) collective-permute-start(bf16[2,2,256,128]{3,2,1,0:T(8,128)(2,1)S(1)} %get-tuple-element.28), channel_id=1, source_target_pairs={{0,1},{1,0},{2,3},{3,2},{4,5},{5,4},{6,7},{7,6},{8,9},{9,8},{10,11... | collective-permute-start | bytes 786440 | tf_op jit(solution)/shard_map/ppermute | solution.py:21
  62.0 0.0 collective-permute-done.4
  62.0 0.4 collective-permute-done.3
  62.4 10.9 %collective-permute-done.6 = bf16[2,2,256,128]{3,2,1,0:T(8,128)(2,1)S(1)} collective-permute-done((bf16[2,2,256,128]{3,2,1,0:T(8,128)(2,1)S(1)}, bf16[2,2,256,128]{3,2,1,0:T(8,128)(2,1)S(1)}, u32[]{:S(2)}, u32[]{:S(2)}) %collective-permute-start.6) | collective-permute-done | bytes 262176 | tf_op jit(solution)/shard_map/ppermute | solution.py:21
  73.3 0.9 pad_maximum_fusion.1
  74.2 0.0 all-to-all-done
  74.2 2.1 %broadcast_in_dim.13 = bf16[16,96,1024]{2,1,0:T(8,128)(2,1)} broadcast(bf16[96,1024]{1,0:T(8,128)(2,1)S(1)} %pad_maximum_fusion.7), dimensions={1,2} | broadcast | bytes 3342336 | tf_op jit(solution)/shard_map/broadcast_in_dim | solution.py:65
  76.3 0.0 copy-done
  76.3 5.5 %all-to-all-start.1 = ((bf16[16,96,1024]{2,1,0:T(8,128)(2,1)}), bf16[16,96,1024]{2,1,0:T(8,128)(2,1)S(1)}, u32[]{:S(2)}, u32[]{:S(2)}) async-start(bf16[16,96,1024]{2,1,0:T(8,128)(2,1)} %broadcast_in_dim.13), calls=%async_computation.1 | async-start | bytes 6291456 | tf_op jit(solution)/shard_map/all_to_all | solution.py:66
  81.8 0.0 copy-start.1
  81.8 1.2 select_bitcast_fusion.1
  83.1 4.0 %collective-permute-start.7 = (bf16[4,512,128]{2,1,0:T(8,128)(2,1)}, bf16[4,512,128]{2,1,0:T(8,128)(2,1)S(1)}, u32[]{:S(2)}, u32[]{:S(2)}) collective-permute-start(bf16[4,512,128]{2,1,0:T(8,128)(2,1)} %bitcast.142), channel_id=1, source_target_pairs={{0,8},{8,0},{1,9},{9,1},{2,10},{10,2},{3,11},{11,3},{4,12},{12,4},... | collective-permute-start | bytes 1572872 | tf_op jit(solution)/shard_map/ppermute | solution.py:21
  87.1 1.2 fusion.19
  88.3 0.3 convolution_add_fusion.4
  88.5 0.3 convolution_add_fusion.3
  88.8 0.0 collective-permute-done.7
  88.8 0.3 fusion.9
  89.1 0.3 fusion.12
  89.3 0.3 fusion.15
  89.6 0.3 fusion.1
  89.9 2.3 %collective-permute-start.8 = (f32[384,128]{1,0:T(8,128)S(1)}, f32[384,128]{1,0:T(8,128)S(1)}, u32[]{:S(2)}, u32[]{:S(2)}) collective-permute-start(f32[384,128]{1,0:T(8,128)S(1)} %fusion.1), channel_id=1, source_target_pairs={{0,8},{8,0},{1,9},{9,1},{2,10},{10,2},{3,11},{11,3},{4,12},{12,4},... | collective-permute-start | bytes 589832 | tf_op jit(solution)/shard_map/ppermute | solution.py:21
  92.1 0.3 convolution_add_fusion.2
  92.4 0.8 collective-permute-done.8
  93.2 4.9 %collective-permute-start.9 = (bf16[2,384,128]{2,1,0:T(8,128)(2,1)S(1)}, bf16[2,384,128]{2,1,0:T(8,128)(2,1)S(1)}, u32[]{:S(2)}, u32[]{:S(2)}) collective-permute-start(bf16[2,384,128]{2,1,0:T(8,128)(2,1)S(1)} %fusion.7), channel_id=1, source_target_pairs={{0,4},{1,5},{2,6},{3,7},{4,0},{5,1},{6,2},{7,3},{8,12},{9,13},{10,... | collective-permute-start | bytes 589832 | tf_op jit(solution)/shard_map/ppermute | solution.py:21
  98.2 18.9 %collective-permute-done.9 = bf16[2,384,128]{2,1,0:T(8,128)(2,1)S(1)} collective-permute-done((bf16[2,384,128]{2,1,0:T(8,128)(2,1)S(1)}, bf16[2,384,128]{2,1,0:T(8,128)(2,1)S(1)}, u32[]{:S(2)}, u32[]{:S(2)}) %collective-permute-start.9) | collective-permute-done | bytes 196640 | tf_op jit(solution)/shard_map/ppermute | solution.py:21
  117.2 0.8 pad_maximum_fusion.4
  117.9 6.9 %all-to-all-done.1 = bf16[16,96,1024]{2,1,0:T(8,128)(2,1)S(1)} async-done(((bf16[16,96,1024]{2,1,0:T(8,128)(2,1)}), bf16[16,96,1024]{2,1,0:T(8,128)(2,1)S(1)}, u32[]{:S(2)}, u32[]{:S(2)}) %all-to-all-start.1) | async-done | bytes 3145760 | tf_op jit(solution)/shard_map/all_to_all | solution.py:66
  124.8 5.1 %collective-permute-start.11 = (bf16[1536,1024]{1,0:T(8,128)(2,1)S(1)}, bf16[1536,1024]{1,0:T(8,128)(2,1)S(1)}, u32[]{:S(2)}, u32[]{:S(2)}) collective-permute-start(bf16[1536,1024]{1,0:T(8,128)(2,1)S(1)} %bitcast.120), channel_id=1, source_target_pairs={{0,8},{8,0},{1,9},{9,1},{2,10},{10,2},{3,11},{11,3},{4,12},{12,4},... | collective-permute-start | bytes 9437192 | tf_op jit(solution)/shard_map/ppermute | solution.py:21
  130.0 4.1 %collective-permute-start.10 = (bf16[2,2,384,128]{3,2,1,0:T(8,128)(2,1)}, bf16[2,2,384,128]{3,2,1,0:T(8,128)(2,1)S(1)}, u32[]{:S(2)}, u32[]{:S(2)}) collective-permute-start(bf16[2,2,384,128]{3,2,1,0:T(8,128)(2,1)} %pad_maximum_fusion.4), channel_id=1, source_target_pairs={{0,1},{1,0},{2,3},{3,2},{4,5},{5,4},{6,7},{7,6},{8,9},{9,8},{10,11... | collective-permute-start | bytes 1179656 | tf_op jit(solution)/shard_map/ppermute | solution.py:21
  134.1 9.7 %collective-permute-done.10 = bf16[2,2,384,128]{3,2,1,0:T(8,128)(2,1)S(1)} collective-permute-done((bf16[2,2,384,128]{3,2,1,0:T(8,128)(2,1)}, bf16[2,2,384,128]{3,2,1,0:T(8,128)(2,1)S(1)}, u32[]{:S(2)}, u32[]{:S(2)}) %collective-permute-start.10) | collective-permute-done | bytes 393248 | tf_op jit(solution)/shard_map/ppermute | solution.py:21
  143.8 1.1 pad_maximum_fusion.2
  144.9 1.0 fusion.44
  145.9 0.0 collective-permute-done.11
  145.9 1.0 fusion.43
  147.0 1.9 collective-permute-start.12
  148.9 13.8 %collective-permute-done.12 = bf16[1024,128]{1,0:T(8,128)(2,1)S(1)} collective-permute-done((bf16[1024,128]{1,0:T(8,128)(2,1)S(1)}, bf16[1024,128]{1,0:T(8,128)(2,1)S(1)}, u32[]{:S(2)}, u32[]{:S(2)}) %collective-permute-start.12) | collective-permute-done | bytes 262176 | tf_op jit(solution)/shard_map/ppermute | solution.py:21
  162.6 1.0 fusion.38
  163.6 1.0 fusion.39
  164.6 0.1 pad_maximum_fusion
  164.7 0.1 fusion.4
  164.8 2.1 %collective-permute-start.13 = (bf16[2,2,384,128]{3,2,0,1:T(8,128)(2,1)S(1)}, bf16[2,2,384,128]{3,2,0,1:T(8,128)(2,1)S(1)}, u32[]{:S(2)}, u32[]{:S(2)}) collective-permute-start(bf16[2,2,384,128]{3,2,0,1:T(8,128)(2,1)S(1)} %fusion.4), channel_id=1, source_target_pairs={{0,1},{1,0},{2,3},{3,2},{4,5},{5,4},{6,7},{7,6},{8,9},{9,8},{10,11... | collective-permute-start | bytes 1179656 | tf_op jit(solution)/shard_map/ppermute | solution.py:21
  166.9 9.1 %collective-permute-done.13 = bf16[2,2,384,128]{3,2,0,1:T(8,128)(2,1)S(1)} collective-permute-done((bf16[2,2,384,128]{3,2,0,1:T(8,128)(2,1)S(1)}, bf16[2,2,384,128]{3,2,0,1:T(8,128)(2,1)S(1)}, u32[]{:S(2)}, u32[]{:S(2)}) %collective-permute-start.13) | collective-permute-done | bytes 393248 | tf_op jit(solution)/shard_map/ppermute | solution.py:21
  176.0 0.1 fusion.2
  176.1 5.9 %collective-permute-start.14 = (bf16[2,384,128]{2,1,0:T(8,128)(2,1)S(1)}, bf16[2,384,128]{2,1,0:T(8,128)(2,1)S(1)}, u32[]{:S(2)}, u32[]{:S(2)}) collective-permute-start(bf16[2,384,128]{2,1,0:T(8,128)(2,1)S(1)} %fusion.29), channel_id=1, source_target_pairs={{0,4},{1,5},{2,6},{3,7},{4,0},{5,1},{6,2},{7,3},{8,12},{9,13},{10,... | collective-permute-start | bytes 589832 | tf_op jit(solution)/shard_map/ppermute | solution.py:21
  182.0 19.4 %collective-permute-done.14 = bf16[2,384,128]{2,1,0:T(8,128)(2,1)S(1)} collective-permute-done((bf16[2,384,128]{2,1,0:T(8,128)(2,1)S(1)}, bf16[2,384,128]{2,1,0:T(8,128)(2,1)S(1)}, u32[]{:S(2)}, u32[]{:S(2)}) %collective-permute-start.14) | collective-permute-done | bytes 196640 | tf_op jit(solution)/shard_map/ppermute | solution.py:21
  201.4 0.0 copy-done.5
  201.4 0.1 fusion.6
  201.5 0.8 copy.17
  (27 shorter events, 0.4 us)
Async XLA Ops:
  0.0 26.7 %collective-permute-start.1 = (bf16[96,256]{1,0:T(8,128)(2,1)}, bf16[96,256]{1,0:T(8,128)(2,1)S(1)}, u32[]{:S(2)}, u32[]{:S(2)}) collective-permute-start(bf16[96,256]{1,0:T(8,128)(2,1)} %bitcast.159), channel_id=1, source_target_pairs={{0,0},{1,64},{2,128},{3,192},{4,256},{5,320},{6,384},{7,448},{64,1... | collective-permute-start | bytes 147464 | tf_op jit(solution)/shard_map/ppermute | solution.py:21
  1.4 25.2 %collective-permute-start = (bf16[96,256]{1,0:T(8,128)(2,1)}, bf16[96,256]{1,0:T(8,128)(2,1)S(1)}, u32[]{:S(2)}, u32[]{:S(2)}) collective-permute-start(bf16[96,256]{1,0:T(8,128)(2,1)} %bitcast.160), channel_id=1, source_target_pairs={{0,64},{1,0},{2,192},{3,128},{4,320},{5,256},{6,448},{7,384},{64,6... | collective-permute-start | bytes 147464 | tf_op jit(solution)/shard_map/ppermute | solution.py:21
  21.8 14.5 %collective-permute-start.2 = (bf16[256,128]{1,0:T(8,128)(2,1)S(1)}, bf16[256,128]{1,0:T(8,128)(2,1)S(1)}, u32[]{:S(2)}, u32[]{:S(2)}) collective-permute-start(bf16[256,128]{1,0:T(8,128)(2,1)S(1)} %pad_maximum_fusion.10), channel_id=1, source_target_pairs={{0,4},{1,5},{2,6},{3,7},{4,0},{5,1},{6,2},{7,3},{8,12},{9,13},{10,... | collective-permute-start | bytes 196616 | tf_op jit(solution)/shard_map/ppermute | solution.py:21
  37.6 7.1 %copy-start.7 = (bf16[96,512]{1,0:T(8,128)(2,1)S(1)}, bf16[96,512]{1,0:T(8,128)(2,1)}, u32[]{:S(2)}) copy-start(bf16[96,512]{1,0:T(8,128)(2,1)} %param.8) | copy-start | bytes 294916
  37.6 36.5 %all-to-all-start = ((bf16[16,96,512]{2,1,0:T(8,128)(2,1)}), bf16[16,96,512]{2,1,0:T(8,128)(2,1)S(1)}, u32[]{:S(2)}, u32[]{:S(2)}) async-start(bf16[16,96,512]{2,1,0:T(8,128)(2,1)} %broadcast_in_dim.12), calls=%async_computation | async-start | bytes 3145728 | tf_op jit(solution)/shard_map/all_to_all | solution.py:66
  41.9 17.9 %collective-permute-start.5 = (bf16[2,256,128]{2,1,0:T(8,128)(2,1)S(1)}, bf16[2,256,128]{2,1,0:T(8,128)(2,1)S(1)}, u32[]{:S(2)}, u32[]{:S(2)}) collective-permute-start(bf16[2,256,128]{2,1,0:T(8,128)(2,1)S(1)} %get-tuple-element.32), channel_id=1, source_target_pairs={{0,2},{1,3},{2,0},{3,1},{4,6},{5,7},{6,4},{7,5},{8,10},{9,11},{10,... | collective-permute-start | bytes 393224 | tf_op jit(solution)/shard_map/ppermute | solution.py:21
  44.7 17.3 %collective-permute-start.4 = (bf16[96,512]{1,0:T(8,128)(2,1)S(1)}, bf16[96,512]{1,0:T(8,128)(2,1)S(1)}, u32[]{:S(2)}, u32[]{:S(2)}) collective-permute-start(bf16[96,512]{1,0:T(8,128)(2,1)S(1)} %copy-done.7), channel_id=1, source_target_pairs={{0,0},{1,129},{2,64},{3,193},{4,260},{5,389},{6,324},{7,453},{64,1... | collective-permute-start | bytes 294920 | tf_op jit(solution)/shard_map/ppermute | solution.py:21
  45.4 17.0 %collective-permute-start.3 = (bf16[96,512]{1,0:T(8,128)(2,1)S(1)}, bf16[96,512]{1,0:T(8,128)(2,1)S(1)}, u32[]{:S(2)}, u32[]{:S(2)}) collective-permute-start(bf16[96,512]{1,0:T(8,128)(2,1)S(1)} %copy-done.7), channel_id=1, source_target_pairs={{0,64},{1,193},{2,0},{3,129},{4,324},{5,453},{6,260},{7,389},{64,1... | collective-permute-start | bytes 294920 | tf_op jit(solution)/shard_map/ppermute | solution.py:21
  59.9 13.5 %collective-permute-start.6 = (bf16[2,2,256,128]{3,2,1,0:T(8,128)(2,1)S(1)}, bf16[2,2,256,128]{3,2,1,0:T(8,128)(2,1)S(1)}, u32[]{:S(2)}, u32[]{:S(2)}) collective-permute-start(bf16[2,2,256,128]{3,2,1,0:T(8,128)(2,1)S(1)} %get-tuple-element.28), channel_id=1, source_target_pairs={{0,1},{1,0},{2,3},{3,2},{4,5},{5,4},{6,7},{7,6},{8,9},{9,8},{10,11... | collective-permute-start | bytes 786440 | tf_op jit(solution)/shard_map/ppermute | solution.py:21
  74.2 2.1 %copy-start = (bf16[16,96,512]{2,1,0:T(8,128)(2,1)}, bf16[16,96,512]{2,1,0:T(8,128)(2,1)S(1)}, u32[]{:S(2)}) copy-start(bf16[16,96,512]{2,1,0:T(8,128)(2,1)S(1)} %all-to-all-done) | copy-start | bytes 4718596
  76.3 48.5 %all-to-all-start.1 = ((bf16[16,96,1024]{2,1,0:T(8,128)(2,1)}), bf16[16,96,1024]{2,1,0:T(8,128)(2,1)S(1)}, u32[]{:S(2)}, u32[]{:S(2)}) async-start(bf16[16,96,1024]{2,1,0:T(8,128)(2,1)} %broadcast_in_dim.13), calls=%async_computation.1 | async-start | bytes 6291456 | tf_op jit(solution)/shard_map/all_to_all | solution.py:66
  81.8 5.2 %copy-start.1 = (bf16[16,96,512]{2,1,0:T(8,128)(2,1)S(1)}, bf16[16,96,512]{2,1,0:T(8,128)(2,1)}, u32[]{:S(2)}) copy-start(bf16[16,96,512]{2,1,0:T(8,128)(2,1)} %copy-done) | copy-start | bytes 4718596
  81.8 6.4 %copy-start.6 = (bf16[2,2,2,256,128]{4,3,2,1,0:T(8,128)(2,1)S(1)}, bf16[2,2,2,256,128]{4,3,2,1,0:T(8,128)(2,1)}, u32[]{:S(2)}) copy-start(bf16[2,2,2,256,128]{4,3,2,1,0:T(8,128)(2,1)} %pad_maximum_fusion.1) | copy-start | bytes 1572868
  83.1 5.7 %collective-permute-start.7 = (bf16[4,512,128]{2,1,0:T(8,128)(2,1)}, bf16[4,512,128]{2,1,0:T(8,128)(2,1)S(1)}, u32[]{:S(2)}, u32[]{:S(2)}) collective-permute-start(bf16[4,512,128]{2,1,0:T(8,128)(2,1)} %bitcast.142), channel_id=1, source_target_pairs={{0,8},{8,0},{1,9},{9,1},{2,10},{10,2},{3,11},{11,3},{4,12},{12,4},... | collective-permute-start | bytes 1572872 | tf_op jit(solution)/shard_map/ppermute | solution.py:21
  89.9 3.3 %collective-permute-start.8 = (f32[384,128]{1,0:T(8,128)S(1)}, f32[384,128]{1,0:T(8,128)S(1)}, u32[]{:S(2)}, u32[]{:S(2)}) collective-permute-start(f32[384,128]{1,0:T(8,128)S(1)} %fusion.1), channel_id=1, source_target_pairs={{0,8},{8,0},{1,9},{9,1},{2,10},{10,2},{3,11},{11,3},{4,12},{12,4},... | collective-permute-start | bytes 589832 | tf_op jit(solution)/shard_map/ppermute | solution.py:21
  92.4 24.8 %copy-start.2 = (f32[384,128]{1,0:T(8,128)}, f32[384,128]{1,0:T(8,128)S(1)}, u32[]{:S(2)}) copy-start(f32[384,128]{1,0:T(8,128)S(1)} %convolution_add_fusion.2) | copy-start | bytes 589828
  93.2 24.0 %copy-start.4 = (f32[384,128]{1,0:T(8,128)}, f32[384,128]{1,0:T(8,128)S(1)}, u32[]{:S(2)}) copy-start(f32[384,128]{1,0:T(8,128)S(1)} %collective-permute-done.8) | copy-start | bytes 589828
  93.2 23.9 %collective-permute-start.9 = (bf16[2,384,128]{2,1,0:T(8,128)(2,1)S(1)}, bf16[2,384,128]{2,1,0:T(8,128)(2,1)S(1)}, u32[]{:S(2)}, u32[]{:S(2)}) collective-permute-start(bf16[2,384,128]{2,1,0:T(8,128)(2,1)S(1)} %fusion.7), channel_id=1, source_target_pairs={{0,4},{1,5},{2,6},{3,7},{4,0},{5,1},{6,2},{7,3},{8,12},{9,13},{10,... | collective-permute-start | bytes 589832 | tf_op jit(solution)/shard_map/ppermute | solution.py:21
  124.8 21.1 %collective-permute-start.11 = (bf16[1536,1024]{1,0:T(8,128)(2,1)S(1)}, bf16[1536,1024]{1,0:T(8,128)(2,1)S(1)}, u32[]{:S(2)}, u32[]{:S(2)}) collective-permute-start(bf16[1536,1024]{1,0:T(8,128)(2,1)S(1)} %bitcast.120), channel_id=1, source_target_pairs={{0,8},{8,0},{1,9},{9,1},{2,10},{10,2},{3,11},{11,3},{4,12},{12,4},... | collective-permute-start | bytes 9437192 | tf_op jit(solution)/shard_map/ppermute | solution.py:21
  130.0 13.8 %collective-permute-start.10 = (bf16[2,2,384,128]{3,2,1,0:T(8,128)(2,1)}, bf16[2,2,384,128]{3,2,1,0:T(8,128)(2,1)S(1)}, u32[]{:S(2)}, u32[]{:S(2)}) collective-permute-start(bf16[2,2,384,128]{3,2,1,0:T(8,128)(2,1)} %pad_maximum_fusion.4), channel_id=1, source_target_pairs={{0,1},{1,0},{2,3},{3,2},{4,5},{5,4},{6,7},{7,6},{8,9},{9,8},{10,11... | collective-permute-start | bytes 1179656 | tf_op jit(solution)/shard_map/ppermute | solution.py:21
  147.0 15.7 %collective-permute-start.12 = (bf16[1024,128]{1,0:T(8,128)(2,1)S(1)}, bf16[1024,128]{1,0:T(8,128)(2,1)S(1)}, u32[]{:S(2)}, u32[]{:S(2)}) collective-permute-start(bf16[1024,128]{1,0:T(8,128)(2,1)S(1)} %get-tuple-element.39), channel_id=1, source_target_pairs={{0,2},{1,3},{2,0},{3,1},{4,6},{5,7},{6,4},{7,5},{8,10},{9,11},{10,... | collective-permute-start | bytes 786440 | tf_op jit(solution)/shard_map/ppermute | solution.py:21
  164.7 36.6 %copy-start.3 = (f32[384,128]{1,0:T(8,128)S(1)}, f32[384,128]{1,0:T(8,128)}, u32[]{:S(2)}) copy-start(f32[384,128]{1,0:T(8,128)} %copy-done.2) | copy-start | bytes 589828
  164.7 36.6 %copy-start.5 = (f32[384,128]{1,0:T(8,128)S(1)}, f32[384,128]{1,0:T(8,128)}, u32[]{:S(2)}) copy-start(f32[384,128]{1,0:T(8,128)} %copy-done.4) | copy-start | bytes 589828
  164.8 11.2 %collective-permute-start.13 = (bf16[2,2,384,128]{3,2,0,1:T(8,128)(2,1)S(1)}, bf16[2,2,384,128]{3,2,0,1:T(8,128)(2,1)S(1)}, u32[]{:S(2)}, u32[]{:S(2)}) collective-permute-start(bf16[2,2,384,128]{3,2,0,1:T(8,128)(2,1)S(1)} %fusion.4), channel_id=1, source_target_pairs={{0,1},{1,0},{2,3},{3,2},{4,5},{5,4},{6,7},{7,6},{8,9},{9,8},{10,11... | collective-permute-start | bytes 1179656 | tf_op jit(solution)/shard_map/ppermute | solution.py:21
  176.1 25.3 %collective-permute-start.14 = (bf16[2,384,128]{2,1,0:T(8,128)(2,1)S(1)}, bf16[2,384,128]{2,1,0:T(8,128)(2,1)S(1)}, u32[]{:S(2)}, u32[]{:S(2)}) collective-permute-start(bf16[2,384,128]{2,1,0:T(8,128)(2,1)S(1)} %fusion.29), channel_id=1, source_target_pairs={{0,4},{1,5},{2,6},{3,7},{4,0},{5,1},{6,2},{7,3},{8,12},{9,13},{10,... | collective-permute-start | bytes 589832 | tf_op jit(solution)/shard_map/ppermute | solution.py:21

commit v3 on v2

--- a/solution.py
+++ b/solution.py
@@ -5,7 +5,7 @@
 
 BLOCK = 128
 SIZES = {"y": 4, "half": 2, "x": 4, "core": 2, "z": 8}
-PAIR, FAR, NEAR = 1, 2, 0
+PAIR, FAR, NEAR = 2, 1, 0
 ROUTE = ("y", "half", "z")
 
 
@@ -72,60 +72,58 @@
     rows, width = accumulated.shape
     fence = lax.optimization_barrier
 
+    b0, b1 = (routed(basis, ROUTE, basis_target(s)) for s in (0, 1))
     act_t = activations.T
     a0, a1 = (routed(act_t, ROUTE, act_target(s)) for s in (0, 1))
     grad = masked_grad(hidden_grad, block_rows)
     g4 = swap_z(grad, 2)
-    b0, b1 = (routed(basis, ROUTE, basis_target(s)) for s in (0, 1))
+    b0, b1, a0, a1, grad, g4 = fence((b0, b1, a0, a1, grad, g4))
+    strip = ordered(half == 1, b0, b1, 1)
+    panel = lax.all_gather(strip, ("y", "x", "core"), axis=0, tiled=True)
 
     act_strip = ordered((half ^ (z & 1)) == 1, a0, a1, 1)
-    act_strip, grad, g4 = fence((act_strip, grad, g4))
     act_all = spread(act_strip).reshape(4, -1, act_strip.shape[1])
     g = jnp.stack([grad, g4], axis=0)
     g = jnp.stack([g, swap_z(g, 1)], axis=1)
     g = jnp.stack([g, swap_z(g, 0)], axis=2)
     g = g.reshape(4, -1, width)
-
-    strip = ordered(half == 1, b0, b1, 1)
-    act_all, strip, g = fence((act_all, strip, g))
     g_other = swap_core(g)
-    panel = spread(strip).reshape(-1, strip.shape[1])
+    act_all, g, g_other = fence((act_all, g, g_other))
 
     def product(right):
         total = jnp.zeros((act_all.shape[1], width), f32)
         for i in range(4):
             total = total + jnp.dot(act_all[i], right[i], preferred_element_type=f32)
-        return total
+        return total.reshape(4, 1, -1, width)
 
     theirs = swap_core(product(g_other))
     mine = product(g)
-    split = accumulated.reshape(4, 2, -1, width)
-    added = ordered(core == 1, split[:, 0], split[:, 1], 0).reshape(2, -1, width)
-    gradient = (jnp.stack([mine, theirs]) + added).astype(bf16)
+    gradient = ordered(core == 1, mine, theirs, 1).reshape(rows, width) + accumulated
+    gradient = gradient.astype(bf16)
 
-    wide = jnp.stack([gradient, swap_z(gradient, FAR)], axis=1)
-    wide, panel = fence((wide, panel))
-    panel_other = swap_core(panel)
-    wide = jnp.stack([wide, swap_z(wide, NEAR)], axis=2)
-    wide = wide.reshape(2, -1, width)
+    wide = jnp.stack([gradient, swap_z(gradient, FAR)], axis=0)
+    wide = jnp.stack([wide, swap_z(wide, NEAR)], axis=1)
+    wide = wide.reshape(-1, width)
 
-    def project(left, right):
+    def project(left):
         return lax.dot_general(
-            left, right, (((0,), (0,)), ((), ())), preferred_element_type=f32
+            left, wide, (((0,), (0,)), ((), ())), preferred_element_type=f32
         )
 
-    coeffs = project(panel, wide[0]) + project(panel_other, wide[1])
-    coeffs = (coeffs + swap_z(coeffs.astype(bf16), PAIR).astype(f32)).astype(bf16)
-    removal = jnp.stack(
-        [
-            jnp.dot(p, coeffs, preferred_element_type=f32).reshape(2, 2, -1, width)
-            for p in (panel, panel_other)
-        ]
-    )
-    kept = removal[:, :, 0] + swap_z(removal[:, :, 1].astype(bf16), NEAR).astype(f32)
-    removed = kept[:, 0] + swap_z(kept[:, 1].astype(bf16), FAR).astype(f32)
-    result = (gradient.astype(f32) - removed).reshape(2, 4, 1, -1, width)
-    return ordered(core == 1, result[0], result[1], 1).reshape(rows, width)
+    removal = 0.0
+    sums = []
+    for part in jnp.split(panel, 2, axis=1):
+        coeffs = project(part)
+        sums.append((part, coeffs, swap_z(coeffs.astype(bf16), PAIR)))
+    for part, coeffs, received in sums:
+        coeffs = (coeffs + received.astype(f32)).astype(bf16)
+        removal = removal + jnp.dot(part, coeffs, preferred_element_type=f32)
+    removal = removal.reshape(2, 2, 2, rows // 2, width)
+    near = [swap_z(removal[:, 1, i].astype(bf16), NEAR) for i in range(2)]
+    kept = [removal[:, 0, i] + near[i].astype(f32) for i in range(2)]
+    far = [swap_z(kept[i][1].astype(bf16), FAR) for i in range(2)]
+    removed = [kept[i][0] + far[i].astype(f32) for i in range(2)]
+    return gradient.astype(f32) - jnp.concatenate(removed, axis=0)
 
 
 def solution(mesh):

time: 203 us -> 190 us (0.936)
  waiting for transfers between devices: 99.4 us -> 66.4 us
  between operations: 0.5 us -> 13.8 us
  starting transfers between devices: 83 us -> 91.2 us
  matrix products: 6.95 us -> 9.98 us
  other arithmetic: 6.67 us -> 4.21 us
  local copies, waits for them, and re-layouts: 5.78 us -> 3.4 us
    ppermute x15 -> x17, waiting for transfers between devices: 92.5 us -> 62.7 us  [routed(): lax.ppermute(value, axes, [(flat[c], flat[tuple(target(*c))]) for c in co...]
    all_to_all x2 -> x1, waiting for transfers between devices: 6.89 us -> 0.01 us  [spread(): return lax.all_to_all(copies, ('y', 'x'), 0, 0)]
    all_to_all x2 -> x1, starting transfers between devices: 9.78 us -> 14.6 us  [spread(): return lax.all_to_all(copies, ('y', 'x'), 0, 0)]
    dot_general x4, matrix products: 3.98 us -> 7.92 us  [the longest x2 5.95 us: project(): lax.dot_general(left, wide, (((0,), (0,)), ((), ())), preferred_element_t...]
    all_gather x0 -> x1, waiting for transfers between devices: none -> 3.73 us  [on_device(): panel = lax.all_gather(strip, ('y', 'x', 'core'), axis=0, tiled=True)]
    ppermute x15 -> x17, starting transfers between devices: 73.2 us -> 76.6 us  [routed(): lax.ppermute(value, axes, [(flat[c], flat[tuple(target(*c))]) for c in co...]
    broadcast_in_dim x2 -> x1, local copies, waits for them, and re-layouts: 3.46 us -> 1.3 us  [spread(): copies = jnp.broadcast_to(strip, (16,) + strip.shape)]
  transfers between devices with their start and end apart: 17 -> 19, of which waited for: 10 -> 13; matrix products, arithmetic and copies ran while one was open for 6% -> 6% of each run, Pallas kernels for 0% -> 0%
where the time goes in v3:
time: 190 us; the launch traced here: 189 us
  starting transfers between devices  91.2 us (48%)
  waiting for transfers between devices  66.4 us (35%)
  between operations  13.8 us (7%)
  matrix products  9.98 us (5%)
  other arithmetic  4.21 us (2%)
  local copies, waits for them, and re-layouts  3.4 us (2%)
    ppermute x17, starting transfers between devices, routed(): lax.ppermute(value, axes, [(flat[c], flat[tuple(target(*c))]) for c in co...  76.6 us
    ppermute x17, waiting for transfers between devices, routed(): lax.ppermute(value, axes, [(flat[c], flat[tuple(target(*c))]) for c in co...  62.7 us
    all_to_all x1, starting transfers between devices, spread(): return lax.all_to_all(copies, ('y', 'x'), 0, 0)  14.6 us
    dot_general x2, matrix products, project(): lax.dot_general(left, wide, (((0,), (0,)), ((), ())), preferred_element_t...  5.95 us
  transfers between devices with their start and end apart: 19, of which 13 were waited for; matrix products, arithmetic and copies ran while one was open for 6% of the time, Pallas kernels for 0%

profile of v3, /device:TPU:1, one launch (start us, length us, event | category | flops | bytes accessed | tf_op | source)
XLA Modules:
  0.0 189.0 jit_solution(16087837971763986795)
XLA Ops:
  6.5 0.0 all-gather.2.cloned.1.call-start
  6.5 1.5 collective-permute-start
  8.1 16.6 %collective-permute-start.1 = (bf16[96,512]{1,0:T(8,128)(2,1)}, bf16[96,512]{1,0:T(8,128)(2,1)S(1)}, u32[]{:S(2)}, u32[]{:S(2)}) collective-permute-start(bf16[96,512]{1,0:T(8,128)(2,1)} %param.8), channel_id=1, source_target_pairs={{0,64},{1,193},{2,322},{3,451},{4,0},{5,129},{6,258},{7,387},{64,1... | collective-permute-start | bytes 294920 | tf_op jit(solution)/shard_map/ppermute | solution.py:21
  24.7 1.4 fusion.51
  26.1 1.3 iota_compare_fusion
  27.4 0.9 slice_select_fusion.1
  28.3 2.2 %collective-permute-start.4 = (bf16[256,128]{1,0:T(8,128)(2,1)S(1)}, bf16[256,128]{1,0:T(8,128)(2,1)S(1)}, u32[]{:S(2)}, u32[]{:S(2)}) collective-permute-start(bf16[256,128]{1,0:T(8,128)(2,1)S(1)} %pad_maximum_fusion.8), channel_id=1, source_target_pairs={{0,4},{1,5},{2,6},{3,7},{4,0},{5,1},{6,2},{7,3},{8,12},{9,13},{10,... | collective-permute-start | bytes 196616 | tf_op jit(solution)/shard_map/ppermute | solution.py:21
  30.5 1.5 collective-permute-start.2
  32.0 13.1 %collective-permute-start.3 = (bf16[96,256]{1,0:T(8,128)(2,1)}, bf16[96,256]{1,0:T(8,128)(2,1)S(1)}, u32[]{:S(2)}, u32[]{:S(2)}) collective-permute-start(bf16[96,256]{1,0:T(8,128)(2,1)} %bitcast.129), channel_id=1, source_target_pairs={{0,64},{1,0},{2,192},{3,128},{4,320},{5,256},{6,448},{7,384},{64,6... | collective-permute-start | bytes 147464 | tf_op jit(solution)/shard_map/ppermute | solution.py:21
  45.1 0.0 collective-permute-done.2
  45.1 1.5 collective-permute-done.3
  46.6 0.0 collective-permute-done.4
  46.6 0.0 collective-permute-done
  46.6 0.0 collective-permute-done.1
  46.6 0.7 pad_maximum_fusion.5
  47.3 0.0 all-gather.2.cloned.1.call-update
  47.4 1.3 broadcast_in_dim.9
  48.7 14.6 %all-to-all-start = ((bf16[16,96,512]{2,1,0:T(8,128)(2,1)}), bf16[16,96,512]{2,1,0:T(8,128)(2,1)S(1)}, u32[]{:S(2)}, u32[]{:S(2)}) async-start(bf16[16,96,512]{2,1,0:T(8,128)(2,1)} %broadcast_in_dim.9), calls=%async_computation | async-start | bytes 3145728 | tf_op jit(solution)/shard_map/all_to_all | solution.py:66
  63.3 1.9 %collective-permute-start.5 = (bf16[2,256,128]{2,1,0:T(8,128)(2,1)S(1)}, bf16[2,256,128]{2,1,0:T(8,128)(2,1)S(1)}, u32[]{:S(2)}, u32[]{:S(2)}) collective-permute-start(bf16[2,256,128]{2,1,0:T(8,128)(2,1)S(1)} %get-tuple-element.36), channel_id=1, source_target_pairs={{0,2},{1,3},{2,0},{3,1},{4,6},{5,7},{6,4},{7,5},{8,10},{9,11},{10,... | collective-permute-start | bytes 393224 | tf_op jit(solution)/shard_map/ppermute | solution.py:21
  65.2 4.7 %collective-permute-done.5 = bf16[2,256,128]{2,1,0:T(8,128)(2,1)S(1)} collective-permute-done((bf16[2,256,128]{2,1,0:T(8,128)(2,1)S(1)}, bf16[2,256,128]{2,1,0:T(8,128)(2,1)S(1)}, u32[]{:S(2)}, u32[]{:S(2)}) %collective-permute-start.5) | collective-permute-done | bytes 131104 | tf_op jit(solution)/shard_map/ppermute | solution.py:21
  70.0 1.9 %collective-permute-start.6 = (bf16[2,2,256,128]{3,2,1,0:T(8,128)(2,1)S(1)}, bf16[2,2,256,128]{3,2,1,0:T(8,128)(2,1)S(1)}, u32[]{:S(2)}, u32[]{:S(2)}) collective-permute-start(bf16[2,2,256,128]{3,2,1,0:T(8,128)(2,1)S(1)} %get-tuple-element.32), channel_id=1, source_target_pairs={{0,1},{1,0},{2,3},{3,2},{4,5},{5,4},{6,7},{7,6},{8,9},{9,8},{10,11... | collective-permute-start | bytes 786440 | tf_op jit(solution)/shard_map/ppermute | solution.py:21
  71.9 5.6 %collective-permute-done.6 = bf16[2,2,256,128]{3,2,1,0:T(8,128)(2,1)S(1)} collective-permute-done((bf16[2,2,256,128]{3,2,1,0:T(8,128)(2,1)S(1)}, bf16[2,2,256,128]{3,2,1,0:T(8,128)(2,1)S(1)}, u32[]{:S(2)}, u32[]{:S(2)}) %collective-permute-start.6) | collective-permute-done | bytes 262176 | tf_op jit(solution)/shard_map/ppermute | solution.py:21
  77.5 0.1 pad_maximum_fusion.1
  77.5 7.0 %collective-permute-start.7 = (bf16[4,512,128]{2,1,0:T(8,128)(2,1)S(1)}, bf16[4,512,128]{2,1,0:T(8,128)(2,1)S(1)}, u32[]{:S(2)}, u32[]{:S(2)}) collective-permute-start(bf16[4,512,128]{2,1,0:T(8,128)(2,1)S(1)} %bitcast.113), channel_id=1, source_target_pairs={{0,8},{8,0},{1,9},{9,1},{2,10},{10,2},{3,11},{11,3},{4,12},{12,4},... | collective-permute-start | bytes 1572872 | tf_op jit(solution)/shard_map/ppermute | solution.py:21
  84.6 1.5 collective-permute-done.7
  86.1 0.0 all-to-all-done
  86.1 0.3 fusion.18
  86.4 0.3 convolution_add_fusion.6
  86.6 0.3 convolution_add_fusion.5
  86.9 0.3 convolution_add_fusion.4
  87.2 6.1 %collective-permute-start.8 = (f32[4,1,96,128]{3,2,0,1:T(8,128)S(1)}, f32[4,1,96,128]{3,2,0,1:T(8,128)S(1)}, u32[]{:S(2)}, u32[]{:S(2)}) collective-permute-start(f32[4,1,96,128]{3,2,0,1:T(8,128)S(1)} %bitcast.124), channel_id=1, source_target_pairs={{0,8},{8,0},{1,9},{9,1},{2,10},{10,2},{3,11},{11,3},{4,12},{12,4},... | collective-permute-start | bytes 589832 | tf_op jit(solution)/shard_map/ppermute | solution.py:21
  93.3 0.3 fusion.16
  93.5 0.3 convolution_add_fusion.3
  93.8 0.3 convolution_add_fusion.2
  94.1 0.0 copy-start.1
  94.1 0.3 convolution_add_fusion.1
  94.3 0.0 collective-permute-done.8
  94.4 0.6 copy-done.1
  95.1 1.9 %collective-permute-start.9 = (bf16[768,128]{1,0:T(8,128)(2,1)S(1)}, bf16[768,128]{1,0:T(8,128)(2,1)S(1)}, u32[]{:S(2)}, u32[]{:S(2)}) collective-permute-start(bf16[768,128]{1,0:T(8,128)(2,1)S(1)} %fusion.9), channel_id=1, source_target_pairs={{0,2},{1,3},{2,0},{3,1},{4,6},{5,7},{6,4},{7,5},{8,10},{9,11},{10,... | collective-permute-start | bytes 589832 | tf_op jit(solution)/shard_map/ppermute | solution.py:21
  97.0 9.8 %collective-permute-done.9 = bf16[768,128]{1,0:T(8,128)(2,1)S(1)} collective-permute-done((bf16[768,128]{1,0:T(8,128)(2,1)S(1)}, bf16[768,128]{1,0:T(8,128)(2,1)S(1)}, u32[]{:S(2)}, u32[]{:S(2)}) %collective-permute-start.9) | collective-permute-done | bytes 196640 | tf_op jit(solution)/shard_map/ppermute | solution.py:21
  106.8 0.1 fusion.50
  106.8 1.9 %collective-permute-start.10 = (bf16[2,768,128]{2,1,0:T(8,128)(2,1)S(1)}, bf16[2,768,128]{2,1,0:T(8,128)(2,1)S(1)}, u32[]{:S(2)}, u32[]{:S(2)}) collective-permute-start(bf16[2,768,128]{2,1,0:T(8,128)(2,1)S(1)} %get-tuple-element.28), channel_id=1, source_target_pairs={{0,1},{1,0},{2,3},{3,2},{4,5},{5,4},{6,7},{7,6},{8,9},{9,8},{10,11... | collective-permute-start | bytes 1179656 | tf_op jit(solution)/shard_map/ppermute | solution.py:21
  108.8 10.3 %collective-permute-done.10 = bf16[2,768,128]{2,1,0:T(8,128)(2,1)S(1)} collective-permute-done((bf16[2,768,128]{2,1,0:T(8,128)(2,1)S(1)}, bf16[2,768,128]{2,1,0:T(8,128)(2,1)S(1)}, u32[]{:S(2)}, u32[]{:S(2)}) %collective-permute-start.10) | collective-permute-done | bytes 393248 | tf_op jit(solution)/shard_map/ppermute | solution.py:21
  119.1 0.1 pad_maximum_fusion
  119.2 3.7 %all-gather.2.cloned.1.call-done = bf16[3072,1024]{1,0:T(8,128)(2,1)} async-done(((bf16[96,1024]{1,0:T(8,128)(2,1)}), bf16[3072,1024]{1,0:T(8,128)(2,1)}) %all-gather.2.cloned.1.call-update) | async-done | bytes 6291472 | tf_op jit(solution)/shard_map/all_gather | solution.py:82
  122.9 3.1 %fusion.52 = (bf16[512,128]{1,0:T(8,128)(2,1)S(1)}, f32[512,128]{1,0:T(8,128)S(1)}) fusion(bf16[3072,128]{1,0:T(8,128)(2,1)S(1)} %bitcast.118, bf16[3072,1024]{1,0:T(8,128)(2,1)} %all-gather.2.cloned.1.call-done), kind=kOutput, calls=%fused_computation.91 | convolution fusion | flops 402718720 | bytes 4325376 | tf_op jit(solution)/shard_map/dot_general | solution.py:109
  126.0 7.4 %collective-permute-start.12 = (bf16[512,128]{1,0:T(8,128)(2,1)S(1)}, bf16[512,128]{1,0:T(8,128)(2,1)S(1)}, u32[]{:S(2)}, u32[]{:S(2)}) collective-permute-start(bf16[512,128]{1,0:T(8,128)(2,1)S(1)} %get-tuple-element.43), channel_id=1, source_target_pairs={{0,4},{1,5},{2,6},{3,7},{4,0},{5,1},{6,2},{7,3},{8,12},{9,13},{10,... | collective-permute-start | bytes 393224 | tf_op jit(solution)/shard_map/ppermute | solution.py:21
  133.3 2.9 %fusion.53 = (bf16[512,128]{1,0:T(8,128)(2,1)S(1)}, f32[512,128]{1,0:T(8,128)S(1)}) fusion(bf16[3072,128]{1,0:T(8,128)(2,1)S(1)} %bitcast.119, bf16[3072,1024]{1,0:T(8,128)(2,1)} %all-gather.2.cloned.1.call-done), kind=kOutput, calls=%fused_computation.92 | convolution fusion | flops 402718720 | bytes 4325376 | tf_op jit(solution)/shard_map/dot_general | solution.py:109
  136.2 1.9 %collective-permute-start.11 = (bf16[512,128]{1,0:T(8,128)(2,1)S(1)}, bf16[512,128]{1,0:T(8,128)(2,1)S(1)}, u32[]{:S(2)}, u32[]{:S(2)}) collective-permute-start(bf16[512,128]{1,0:T(8,128)(2,1)S(1)} %get-tuple-element.45), channel_id=1, source_target_pairs={{0,4},{1,5},{2,6},{3,7},{4,0},{5,1},{6,2},{7,3},{8,12},{9,13},{10,... | collective-permute-start | bytes 393224 | tf_op jit(solution)/shard_map/ppermute | solution.py:21
  138.2 7.1 %collective-permute-done.12 = bf16[512,128]{1,0:T(8,128)(2,1)S(1)} collective-permute-done((bf16[512,128]{1,0:T(8,128)(2,1)S(1)}, bf16[512,128]{1,0:T(8,128)(2,1)S(1)}, u32[]{:S(2)}, u32[]{:S(2)}) %collective-permute-start.12) | collective-permute-done | bytes 131104 | tf_op jit(solution)/shard_map/ppermute | solution.py:21
  145.2 1.0 fusion
  146.2 10.2 %collective-permute-done.11 = bf16[512,128]{1,0:T(8,128)(2,1)S(1)} collective-permute-done((bf16[512,128]{1,0:T(8,128)(2,1)S(1)}, bf16[512,128]{1,0:T(8,128)(2,1)S(1)}, u32[]{:S(2)}, u32[]{:S(2)}) %collective-permute-start.11) | collective-permute-done | bytes 131104 | tf_op jit(solution)/shard_map/ppermute | solution.py:21
  156.5 1.0 convolution_add_fusion
  157.4 0.1 slice_bitcast_fusion.5
  157.5 1.9 %collective-permute-start.13 = (bf16[2,384,128]{2,1,0:T(8,128)(2,1)S(1)}, bf16[2,384,128]{2,1,0:T(8,128)(2,1)S(1)}, u32[]{:S(2)}, u32[]{:S(2)}) collective-permute-start(bf16[2,384,128]{2,1,0:T(8,128)(2,1)S(1)} %get-tuple-element.25), channel_id=1, source_target_pairs={{0,1},{1,0},{2,3},{3,2},{4,5},{5,4},{6,7},{7,6},{8,9},{9,8},{10,11... | collective-permute-start | bytes 589832 | tf_op jit(solution)/shard_map/ppermute | solution.py:21
  159.4 3.4 %collective-permute-start.15 = (bf16[2,384,128]{2,1,0:T(8,128)(2,1)S(1)}, bf16[2,384,128]{2,1,0:T(8,128)(2,1)S(1)}, u32[]{:S(2)}, u32[]{:S(2)}) collective-permute-start(bf16[2,384,128]{2,1,0:T(8,128)(2,1)S(1)} %get-tuple-element.26), channel_id=1, source_target_pairs={{0,1},{1,0},{2,3},{3,2},{4,5},{5,4},{6,7},{7,6},{8,9},{9,8},{10,11... | collective-permute-start | bytes 589832 | tf_op jit(solution)/shard_map/ppermute | solution.py:21
  162.8 2.0 %collective-permute-done.13 = bf16[2,384,128]{2,1,0:T(8,128)(2,1)S(1)} collective-permute-done((bf16[2,384,128]{2,1,0:T(8,128)(2,1)S(1)}, bf16[2,384,128]{2,1,0:T(8,128)(2,1)S(1)}, u32[]{:S(2)}, u32[]{:S(2)}) %collective-permute-start.13) | collective-permute-done | bytes 196640 | tf_op jit(solution)/shard_map/ppermute | solution.py:21
  164.8 4.2 %collective-permute-done.15 = bf16[2,384,128]{2,1,0:T(8,128)(2,1)S(1)} collective-permute-done((bf16[2,384,128]{2,1,0:T(8,128)(2,1)S(1)}, bf16[2,384,128]{2,1,0:T(8,128)(2,1)S(1)}, u32[]{:S(2)}, u32[]{:S(2)}) %collective-permute-start.15) | collective-permute-done | bytes 196640 | tf_op jit(solution)/shard_map/ppermute | solution.py:21
  169.1 0.1 fusion.8
  169.2 4.4 %collective-permute-start.14 = (bf16[384,128]{1,0:T(8,128)(2,1)S(1)}, bf16[384,128]{1,0:T(8,128)(2,1)S(1)}, u32[]{:S(2)}, u32[]{:S(2)}) collective-permute-start(bf16[384,128]{1,0:T(8,128)(2,1)S(1)} %fusion.46), channel_id=1, source_target_pairs={{0,2},{1,3},{2,0},{3,1},{4,6},{5,7},{6,4},{7,5},{8,10},{9,11},{10,... | collective-permute-start | bytes 294920 | tf_op jit(solution)/shard_map/ppermute | solution.py:21
  173.6 1.9 %collective-permute-start.16 = (bf16[384,128]{1,0:T(8,128)(2,1)S(1)}, bf16[384,128]{1,0:T(8,128)(2,1)S(1)}, u32[]{:S(2)}, u32[]{:S(2)}) collective-permute-start(bf16[384,128]{1,0:T(8,128)(2,1)S(1)} %fusion.47), channel_id=1, source_target_pairs={{0,2},{1,3},{2,0},{3,1},{4,6},{5,7},{6,4},{7,5},{8,10},{9,11},{10,... | collective-permute-start | bytes 294920 | tf_op jit(solution)/shard_map/ppermute | solution.py:21
  175.5 1.1 collective-permute-done.14
  176.6 4.7 %collective-permute-done.16 = bf16[384,128]{1,0:T(8,128)(2,1)S(1)} collective-permute-done((bf16[384,128]{1,0:T(8,128)(2,1)S(1)}, bf16[384,128]{1,0:T(8,128)(2,1)S(1)}, u32[]{:S(2)}, u32[]{:S(2)}) %collective-permute-start.16) | collective-permute-done | bytes 98336 | tf_op jit(solution)/shard_map/ppermute | solution.py:21
  181.3 0.8 maximum_subtract_fusion
  (16 shorter events, 0.3 us)
Async XLA Ops:
  6.5 116.4 %all-gather.2.cloned.1.call-start = ((), (), s32[]{:S(2)}) async-start(), calls=%async_computation.1 | async-start | bytes 6488064 | tf_op jit(solution)/shard_map/all_gather | solution.py:82
  6.5 40.1 %collective-permute-start = (bf16[96,512]{1,0:T(8,128)(2,1)}, bf16[96,512]{1,0:T(8,128)(2,1)S(1)}, u32[]{:S(2)}, u32[]{:S(2)}) collective-permute-start(bf16[96,512]{1,0:T(8,128)(2,1)} %param.8), channel_id=1, source_target_pairs={{0,0},{1,129},{2,258},{3,387},{4,64},{5,193},{6,322},{7,451},{64,1... | collective-permute-start | bytes 294920 | tf_op jit(solution)/shard_map/ppermute | solution.py:21
  8.1 38.5 %collective-permute-start.1 = (bf16[96,512]{1,0:T(8,128)(2,1)}, bf16[96,512]{1,0:T(8,128)(2,1)S(1)}, u32[]{:S(2)}, u32[]{:S(2)}) collective-permute-start(bf16[96,512]{1,0:T(8,128)(2,1)} %param.8), channel_id=1, source_target_pairs={{0,64},{1,193},{2,322},{3,451},{4,0},{5,129},{6,258},{7,387},{64,1... | collective-permute-start | bytes 294920 | tf_op jit(solution)/shard_map/ppermute | solution.py:21
  28.3 18.3 %collective-permute-start.4 = (bf16[256,128]{1,0:T(8,128)(2,1)S(1)}, bf16[256,128]{1,0:T(8,128)(2,1)S(1)}, u32[]{:S(2)}, u32[]{:S(2)}) collective-permute-start(bf16[256,128]{1,0:T(8,128)(2,1)S(1)} %pad_maximum_fusion.8), channel_id=1, source_target_pairs={{0,4},{1,5},{2,6},{3,7},{4,0},{5,1},{6,2},{7,3},{8,12},{9,13},{10,... | collective-permute-start | bytes 196616 | tf_op jit(solution)/shard_map/ppermute | solution.py:21
  30.5 14.6 %collective-permute-start.2 = (bf16[96,256]{1,0:T(8,128)(2,1)}, bf16[96,256]{1,0:T(8,128)(2,1)S(1)}, u32[]{:S(2)}, u32[]{:S(2)}) collective-permute-start(bf16[96,256]{1,0:T(8,128)(2,1)} %bitcast.128), channel_id=1, source_target_pairs={{0,0},{1,64},{2,128},{3,192},{4,256},{5,320},{6,384},{7,448},{64,1... | collective-permute-start | bytes 147464 | tf_op jit(solution)/shard_map/ppermute | solution.py:21
  32.0 14.6 %collective-permute-start.3 = (bf16[96,256]{1,0:T(8,128)(2,1)}, bf16[96,256]{1,0:T(8,128)(2,1)S(1)}, u32[]{:S(2)}, u32[]{:S(2)}) collective-permute-start(bf16[96,256]{1,0:T(8,128)(2,1)} %bitcast.129), channel_id=1, source_target_pairs={{0,64},{1,0},{2,192},{3,128},{4,320},{5,256},{6,448},{7,384},{64,6... | collective-permute-start | bytes 147464 | tf_op jit(solution)/shard_map/ppermute | solution.py:21
  48.7 37.4 %all-to-all-start = ((bf16[16,96,512]{2,1,0:T(8,128)(2,1)}), bf16[16,96,512]{2,1,0:T(8,128)(2,1)S(1)}, u32[]{:S(2)}, u32[]{:S(2)}) async-start(bf16[16,96,512]{2,1,0:T(8,128)(2,1)} %broadcast_in_dim.9), calls=%async_computation | async-start | bytes 3145728 | tf_op jit(solution)/shard_map/all_to_all | solution.py:66
  63.3 6.6 %collective-permute-start.5 = (bf16[2,256,128]{2,1,0:T(8,128)(2,1)S(1)}, bf16[2,256,128]{2,1,0:T(8,128)(2,1)S(1)}, u32[]{:S(2)}, u32[]{:S(2)}) collective-permute-start(bf16[2,256,128]{2,1,0:T(8,128)(2,1)S(1)} %get-tuple-element.36), channel_id=1, source_target_pairs={{0,2},{1,3},{2,0},{3,1},{4,6},{5,7},{6,4},{7,5},{8,10},{9,11},{10,... | collective-permute-start | bytes 393224 | tf_op jit(solution)/shard_map/ppermute | solution.py:21
  70.0 7.5 %collective-permute-start.6 = (bf16[2,2,256,128]{3,2,1,0:T(8,128)(2,1)S(1)}, bf16[2,2,256,128]{3,2,1,0:T(8,128)(2,1)S(1)}, u32[]{:S(2)}, u32[]{:S(2)}) collective-permute-start(bf16[2,2,256,128]{3,2,1,0:T(8,128)(2,1)S(1)} %get-tuple-element.32), channel_id=1, source_target_pairs={{0,1},{1,0},{2,3},{3,2},{4,5},{5,4},{6,7},{7,6},{8,9},{9,8},{10,11... | collective-permute-start | bytes 786440 | tf_op jit(solution)/shard_map/ppermute | solution.py:21
  77.5 8.6 %collective-permute-start.7 = (bf16[4,512,128]{2,1,0:T(8,128)(2,1)S(1)}, bf16[4,512,128]{2,1,0:T(8,128)(2,1)S(1)}, u32[]{:S(2)}, u32[]{:S(2)}) collective-permute-start(bf16[4,512,128]{2,1,0:T(8,128)(2,1)S(1)} %bitcast.113), channel_id=1, source_target_pairs={{0,8},{8,0},{1,9},{9,1},{2,10},{10,2},{3,11},{11,3},{4,12},{12,4},... | collective-permute-start | bytes 1572872 | tf_op jit(solution)/shard_map/ppermute | solution.py:21
  87.2 7.2 %collective-permute-start.8 = (f32[4,1,96,128]{3,2,0,1:T(8,128)S(1)}, f32[4,1,96,128]{3,2,0,1:T(8,128)S(1)}, u32[]{:S(2)}, u32[]{:S(2)}) collective-permute-start(f32[4,1,96,128]{3,2,0,1:T(8,128)S(1)} %bitcast.124), channel_id=1, source_target_pairs={{0,8},{8,0},{1,9},{9,1},{2,10},{10,2},{3,11},{11,3},{4,12},{12,4},... | collective-permute-start | bytes 589832 | tf_op jit(solution)/shard_map/ppermute | solution.py:21
  94.1 1.0 copy-start.1
  95.1 11.7 %collective-permute-start.9 = (bf16[768,128]{1,0:T(8,128)(2,1)S(1)}, bf16[768,128]{1,0:T(8,128)(2,1)S(1)}, u32[]{:S(2)}, u32[]{:S(2)}) collective-permute-start(bf16[768,128]{1,0:T(8,128)(2,1)S(1)} %fusion.9), channel_id=1, source_target_pairs={{0,2},{1,3},{2,0},{3,1},{4,6},{5,7},{6,4},{7,5},{8,10},{9,11},{10,... | collective-permute-start | bytes 589832 | tf_op jit(solution)/shard_map/ppermute | solution.py:21
  106.8 12.3 %collective-permute-start.10 = (bf16[2,768,128]{2,1,0:T(8,128)(2,1)S(1)}, bf16[2,768,128]{2,1,0:T(8,128)(2,1)S(1)}, u32[]{:S(2)}, u32[]{:S(2)}) collective-permute-start(bf16[2,768,128]{2,1,0:T(8,128)(2,1)S(1)} %get-tuple-element.28), channel_id=1, source_target_pairs={{0,1},{1,0},{2,3},{3,2},{4,5},{5,4},{6,7},{7,6},{8,9},{9,8},{10,11... | collective-permute-start | bytes 1179656 | tf_op jit(solution)/shard_map/ppermute | solution.py:21
  122.9 22.3 %copy-start = (bf16[3072,1024]{1,0:T(8,128)(2,1)S(1)}, bf16[3072,1024]{1,0:T(8,128)(2,1)}, u32[]{:S(2)}) copy-start(bf16[3072,1024]{1,0:T(8,128)(2,1)} %all-gather.2.cloned.1.call-done) | copy-start | bytes 18874372
  126.0 19.3 %collective-permute-start.12 = (bf16[512,128]{1,0:T(8,128)(2,1)S(1)}, bf16[512,128]{1,0:T(8,128)(2,1)S(1)}, u32[]{:S(2)}, u32[]{:S(2)}) collective-permute-start(bf16[512,128]{1,0:T(8,128)(2,1)S(1)} %get-tuple-element.43), channel_id=1, source_target_pairs={{0,4},{1,5},{2,6},{3,7},{4,0},{5,1},{6,2},{7,3},{8,12},{9,13},{10,... | collective-permute-start | bytes 393224 | tf_op jit(solution)/shard_map/ppermute | solution.py:21
  136.2 20.2 %collective-permute-start.11 = (bf16[512,128]{1,0:T(8,128)(2,1)S(1)}, bf16[512,128]{1,0:T(8,128)(2,1)S(1)}, u32[]{:S(2)}, u32[]{:S(2)}) collective-permute-start(bf16[512,128]{1,0:T(8,128)(2,1)S(1)} %get-tuple-element.45), channel_id=1, source_target_pairs={{0,4},{1,5},{2,6},{3,7},{4,0},{5,1},{6,2},{7,3},{8,12},{9,13},{10,... | collective-permute-start | bytes 393224 | tf_op jit(solution)/shard_map/ppermute | solution.py:21
  157.5 7.3 %collective-permute-start.13 = (bf16[2,384,128]{2,1,0:T(8,128)(2,1)S(1)}, bf16[2,384,128]{2,1,0:T(8,128)(2,1)S(1)}, u32[]{:S(2)}, u32[]{:S(2)}) collective-permute-start(bf16[2,384,128]{2,1,0:T(8,128)(2,1)S(1)} %get-tuple-element.25), channel_id=1, source_target_pairs={{0,1},{1,0},{2,3},{3,2},{4,5},{5,4},{6,7},{7,6},{8,9},{9,8},{10,11... | collective-permute-start | bytes 589832 | tf_op jit(solution)/shard_map/ppermute | solution.py:21
  159.4 9.6 %collective-permute-start.15 = (bf16[2,384,128]{2,1,0:T(8,128)(2,1)S(1)}, bf16[2,384,128]{2,1,0:T(8,128)(2,1)S(1)}, u32[]{:S(2)}, u32[]{:S(2)}) collective-permute-start(bf16[2,384,128]{2,1,0:T(8,128)(2,1)S(1)} %get-tuple-element.26), channel_id=1, source_target_pairs={{0,1},{1,0},{2,3},{3,2},{4,5},{5,4},{6,7},{7,6},{8,9},{9,8},{10,11... | collective-permute-start | bytes 589832 | tf_op jit(solution)/shard_map/ppermute | solution.py:21
  169.2 7.4 %collective-permute-start.14 = (bf16[384,128]{1,0:T(8,128)(2,1)S(1)}, bf16[384,128]{1,0:T(8,128)(2,1)S(1)}, u32[]{:S(2)}, u32[]{:S(2)}) collective-permute-start(bf16[384,128]{1,0:T(8,128)(2,1)S(1)} %fusion.46), channel_id=1, source_target_pairs={{0,2},{1,3},{2,0},{3,1},{4,6},{5,7},{6,4},{7,5},{8,10},{9,11},{10,... | collective-permute-start | bytes 294920 | tf_op jit(solution)/shard_map/ppermute | solution.py:21
  173.6 7.8 %collective-permute-start.16 = (bf16[384,128]{1,0:T(8,128)(2,1)S(1)}, bf16[384,128]{1,0:T(8,128)(2,1)S(1)}, u32[]{:S(2)}, u32[]{:S(2)}) collective-permute-start(bf16[384,128]{1,0:T(8,128)(2,1)S(1)} %fusion.47), channel_id=1, source_target_pairs={{0,2},{1,3},{2,0},{3,1},{4,6},{5,7},{6,4},{7,5},{8,10},{9,11},{10,... | collective-permute-start | bytes 294920 | tf_op jit(solution)/shard_map/ppermute | solution.py:21
Sparse Core Ops, SparseCore 0:
  47.5 75.3 all-gather.1

commit v4 on v3

--- a/solution.py
+++ b/solution.py
@@ -21,8 +21,12 @@
     return lax.ppermute(value, axes, [(flat[c], flat[tuple(target(*c))]) for c in coords])
 
 
+def flip_z(value, mask):
+    return routed(value, ("z",), lambda z: (z ^ mask,))
+
+
 def swap_z(value, i):
-    return routed(value, ("z",), lambda z: (z ^ (1 << i),))
+    return flip_z(value, 1 << i)
 
 
 def swap_core(value):
@@ -77,11 +81,12 @@
     a0, a1 = (routed(act_t, ROUTE, act_target(s)) for s in (0, 1))
     grad = masked_grad(hidden_grad, block_rows)
     g4 = swap_z(grad, 2)
-    b0, b1, a0, a1, grad, g4 = fence((b0, b1, a0, a1, grad, g4))
+    b0, b1, a0, a1 = fence((b0, b1, a0, a1))
     strip = ordered(half == 1, b0, b1, 1)
     panel = lax.all_gather(strip, ("y", "x", "core"), axis=0, tiled=True)
 
     act_strip = ordered((half ^ (z & 1)) == 1, a0, a1, 1)
+    act_strip, grad, g4 = fence((act_strip, grad, g4))
     act_all = spread(act_strip).reshape(4, -1, act_strip.shape[1])
     g = jnp.stack([grad, g4], axis=0)
     g = jnp.stack([g, swap_z(g, 1)], axis=1)
@@ -101,9 +106,8 @@
     gradient = ordered(core == 1, mine, theirs, 1).reshape(rows, width) + accumulated
     gradient = gradient.astype(bf16)
 
-    wide = jnp.stack([gradient, swap_z(gradient, FAR)], axis=0)
-    wide = jnp.stack([wide, swap_z(wide, NEAR)], axis=1)
-    wide = wide.reshape(-1, width)
+    masks = [1 << NEAR, 1 << FAR, (1 << FAR) | (1 << NEAR)]
+    wide = jnp.concatenate([gradient] + [flip_z(gradient, m) for m in masks], axis=0)
 
     def project(left):
         return lax.dot_general(
@@ -118,12 +122,11 @@
     for part, coeffs, received in sums:
         coeffs = (coeffs + received.astype(f32)).astype(bf16)
         removal = removal + jnp.dot(part, coeffs, preferred_element_type=f32)
-    removal = removal.reshape(2, 2, 2, rows // 2, width)
-    near = [swap_z(removal[:, 1, i].astype(bf16), NEAR) for i in range(2)]
-    kept = [removal[:, 0, i] + near[i].astype(f32) for i in range(2)]
-    far = [swap_z(kept[i][1].astype(bf16), FAR) for i in range(2)]
-    removed = [kept[i][0] + far[i].astype(f32) for i in range(2)]
-    return gradient.astype(f32) - jnp.concatenate(removed, axis=0)
+    removal = removal.reshape(4, rows, width)
+    removed = removal[0]
+    for slot, m in enumerate(masks, 1):
+        removed = removed + flip_z(removal[slot].astype(bf16), m).astype(f32)
+    return gradient.astype(f32) - removed
 
 
 def solution(mesh):

time: 190 us -> 188 us (0.989); the launches traced: 189 us -> 185 us
  waiting for transfers between devices: 66.4 us -> 63.4 us
    ppermute x17, starting transfers between devices: 76.6 us -> 82.7 us  [routed(): lax.ppermute(value, axes, [(flat[c], flat[tuple(target(*c))]) for c in co...]
    all_to_all x1, starting transfers between devices: 14.6 us -> 9.39 us  [spread(): return lax.all_to_all(copies, ('y', 'x'), 0, 0)]
    all_gather x1, waiting for transfers between devices: 3.73 us -> 1.1 us  [on_device(): panel = lax.all_gather(strip, ('y', 'x', 'core'), axis=0, tiled=True)]
  transfers between devices with their start and end apart: 19 -> 19, of which waited for: 13 -> 11; matrix products, arithmetic and copies ran while one was open for 6% -> 5% of each run, Pallas kernels for 0% -> 0%
where the time goes in v4:
time: 188 us; the launch traced here: 185 us
  starting transfers between devices  92.1 us (49%)
  waiting for transfers between devices  63.4 us (34%)
  between operations  13.8 us (7%)
  matrix products  8.09 us (4%)
  other arithmetic  3.87 us (2%)
  local copies, waits for them, and re-layouts  3.31 us (2%)
    ppermute x17, starting transfers between devices, routed(): lax.ppermute(value, axes, [(flat[c], flat[tuple(target(*c))]) for c in co...  82.7 us
    ppermute x17, waiting for transfers between devices, routed(): lax.ppermute(value, axes, [(flat[c], flat[tuple(target(*c))]) for c in co...  62.2 us
    all_to_all x1, starting transfers between devices, spread(): return lax.all_to_all(copies, ('y', 'x'), 0, 0)  9.39 us
    dot_general x2, matrix products, project(): lax.dot_general(left, wide, (((0,), (0,)), ((), ())), preferred_element_t...  4.08 us
  transfers between devices with their start and end apart: 19, of which 11 were waited for; matrix products, arithmetic and copies ran while one was open for 5% of the time, Pallas kernels for 0%

profile of v4, /device:TPU:1, one launch (start us, length us, event | category | flops | bytes accessed | tf_op | source)
XLA Modules:
  0.0 184.5 jit_solution(9461182190636522136)
XLA Ops:
  6.5 0.0 all-gather.2.cloned.1.call-start
  6.5 1.5 collective-permute-start
  8.1 16.6 %collective-permute-start.1 = (bf16[96,512]{1,0:T(8,128)(2,1)}, bf16[96,512]{1,0:T(8,128)(2,1)S(1)}, u32[]{:S(2)}, u32[]{:S(2)}) collective-permute-start(bf16[96,512]{1,0:T(8,128)(2,1)} %param.8), channel_id=1, source_target_pairs={{0,64},{1,193},{2,322},{3,451},{4,0},{5,129},{6,258},{7,387},{64,1... | collective-permute-start | bytes 294920 | tf_op jit(solution)/shard_map/ppermute | solution.py:21
  24.7 1.5 collective-permute-start.2
  26.2 13.1 %collective-permute-start.3 = (bf16[96,256]{1,0:T(8,128)(2,1)}, bf16[96,256]{1,0:T(8,128)(2,1)S(1)}, u32[]{:S(2)}, u32[]{:S(2)}) collective-permute-start(bf16[96,256]{1,0:T(8,128)(2,1)} %bitcast.87), channel_id=1, source_target_pairs={{0,64},{1,0},{2,192},{3,128},{4,320},{5,256},{6,448},{7,384},{64,6... | collective-permute-start | bytes 147464 | tf_op jit(solution)/shard_map/ppermute | solution.py:21
  39.3 0.0 collective-permute-done.2
  39.3 3.9 %collective-permute-done.3 = bf16[96,256]{1,0:T(8,128)(2,1)S(1)} collective-permute-done((bf16[96,256]{1,0:T(8,128)(2,1)}, bf16[96,256]{1,0:T(8,128)(2,1)S(1)}, u32[]{:S(2)}, u32[]{:S(2)}) %collective-permute-start.3) | collective-permute-done | bytes 49184 | tf_op jit(solution)/shard_map/ppermute | solution.py:21
  43.2 0.0 collective-permute-done
  43.2 0.0 collective-permute-done.1
  43.3 0.7 pad_maximum_fusion.4
  43.9 0.0 all-gather.2.cloned.1.call-update
  44.0 1.3 fusion.50
  45.3 1.2 iota_compare_fusion
  46.5 0.9 slice_select_fusion.1
  47.4 1.9 %collective-permute-start.4 = (bf16[256,128]{1,0:T(8,128)(2,1)S(1)}, bf16[256,128]{1,0:T(8,128)(2,1)S(1)}, u32[]{:S(2)}, u32[]{:S(2)}) collective-permute-start(bf16[256,128]{1,0:T(8,128)(2,1)S(1)} %pad_maximum_fusion.9), channel_id=1, source_target_pairs={{0,4},{1,5},{2,6},{3,7},{4,0},{5,1},{6,2},{7,3},{8,12},{9,13},{10,... | collective-permute-start | bytes 196616 | tf_op jit(solution)/shard_map/ppermute | solution.py:21
  49.4 6.9 %collective-permute-done.4 = bf16[256,128]{1,0:T(8,128)(2,1)S(1)} collective-permute-done((bf16[256,128]{1,0:T(8,128)(2,1)S(1)}, bf16[256,128]{1,0:T(8,128)(2,1)S(1)}, u32[]{:S(2)}, u32[]{:S(2)}) %collective-permute-start.4) | collective-permute-done | bytes 65568 | tf_op jit(solution)/shard_map/ppermute | solution.py:21
  56.3 1.3 broadcast_in_dim.9
  57.6 9.4 %all-to-all-start = ((bf16[16,96,512]{2,1,0:T(8,128)(2,1)}), bf16[16,96,512]{2,1,0:T(8,128)(2,1)S(1)}, u32[]{:S(2)}, u32[]{:S(2)}) async-start(bf16[16,96,512]{2,1,0:T(8,128)(2,1)} %broadcast_in_dim.9), calls=%async_computation | async-start | bytes 3145728 | tf_op jit(solution)/shard_map/all_to_all | solution.py:70
  67.0 1.9 %collective-permute-start.5 = (bf16[2,256,128]{2,1,0:T(8,128)(2,1)S(1)}, bf16[2,256,128]{2,1,0:T(8,128)(2,1)S(1)}, u32[]{:S(2)}, u32[]{:S(2)}) collective-permute-start(bf16[2,256,128]{2,1,0:T(8,128)(2,1)S(1)} %get-tuple-element.35), channel_id=1, source_target_pairs={{0,2},{1,3},{2,0},{3,1},{4,6},{5,7},{6,4},{7,5},{8,10},{9,11},{10,... | collective-permute-start | bytes 393224 | tf_op jit(solution)/shard_map/ppermute | solution.py:21
  69.0 5.1 %collective-permute-done.5 = bf16[2,256,128]{2,1,0:T(8,128)(2,1)S(1)} collective-permute-done((bf16[2,256,128]{2,1,0:T(8,128)(2,1)S(1)}, bf16[2,256,128]{2,1,0:T(8,128)(2,1)S(1)}, u32[]{:S(2)}, u32[]{:S(2)}) %collective-permute-start.5) | collective-permute-done | bytes 131104 | tf_op jit(solution)/shard_map/ppermute | solution.py:21
  74.1 6.9 %collective-permute-start.6 = (bf16[2,2,256,128]{3,2,1,0:T(8,128)(2,1)S(1)}, bf16[2,2,256,128]{3,2,1,0:T(8,128)(2,1)S(1)}, u32[]{:S(2)}, u32[]{:S(2)}) collective-permute-start(bf16[2,2,256,128]{3,2,1,0:T(8,128)(2,1)S(1)} %get-tuple-element.31), channel_id=1, source_target_pairs={{0,1},{1,0},{2,3},{3,2},{4,5},{5,4},{6,7},{7,6},{8,9},{9,8},{10,11... | collective-permute-start | bytes 786440 | tf_op jit(solution)/shard_map/ppermute | solution.py:21
  81.0 5.1 %collective-permute-done.6 = bf16[2,2,256,128]{3,2,1,0:T(8,128)(2,1)S(1)} collective-permute-done((bf16[2,2,256,128]{3,2,1,0:T(8,128)(2,1)S(1)}, bf16[2,2,256,128]{3,2,1,0:T(8,128)(2,1)S(1)}, u32[]{:S(2)}, u32[]{:S(2)}) %collective-permute-start.6) | collective-permute-done | bytes 262176 | tf_op jit(solution)/shard_map/ppermute | solution.py:21
  86.1 0.1 pad_maximum_fusion.1
  86.1 4.1 %collective-permute-start.7 = (bf16[4,512,128]{2,1,0:T(8,128)(2,1)S(1)}, bf16[4,512,128]{2,1,0:T(8,128)(2,1)S(1)}, u32[]{:S(2)}, u32[]{:S(2)}) collective-permute-start(bf16[4,512,128]{2,1,0:T(8,128)(2,1)S(1)} %bitcast.75), channel_id=1, source_target_pairs={{0,8},{8,0},{1,9},{9,1},{2,10},{10,2},{3,11},{11,3},{4,12},{12,4},... | collective-permute-start | bytes 1572872 | tf_op jit(solution)/shard_map/ppermute | solution.py:21
  90.2 1.5 collective-permute-done.7
  91.7 0.0 all-to-all-done
  91.7 0.3 fusion.19
  92.0 0.3 convolution_add_fusion.6
  92.3 0.3 convolution_add_fusion.5
  92.5 0.3 convolution_add_fusion.4
  92.8 3.3 %collective-permute-start.8 = (f32[4,1,96,128]{3,2,0,1:T(8,128)S(1)}, f32[4,1,96,128]{3,2,0,1:T(8,128)S(1)}, u32[]{:S(2)}, u32[]{:S(2)}) collective-permute-start(f32[4,1,96,128]{3,2,0,1:T(8,128)S(1)} %bitcast.83), channel_id=1, source_target_pairs={{0,8},{8,0},{1,9},{9,1},{2,10},{10,2},{3,11},{11,3},{4,12},{12,4},... | collective-permute-start | bytes 589832 | tf_op jit(solution)/shard_map/ppermute | solution.py:21
  96.1 0.3 fusion.17
  96.4 0.3 convolution_add_fusion.3
  96.6 0.3 convolution_add_fusion.2
  96.9 0.0 copy-start.1
  96.9 0.3 convolution_add_fusion.1
  97.2 0.0 collective-permute-done.8
  97.3 0.6 copy-done.1
  97.9 2.0 %collective-permute-start.10 = (bf16[768,128]{1,0:T(8,128)(2,1)S(1)}, bf16[768,128]{1,0:T(8,128)(2,1)S(1)}, u32[]{:S(2)}, u32[]{:S(2)}) collective-permute-start(bf16[768,128]{1,0:T(8,128)(2,1)S(1)} %fusion.10), channel_id=1, source_target_pairs={{0,2},{1,3},{2,0},{3,1},{4,6},{5,7},{6,4},{7,5},{8,10},{9,11},{10,... | collective-permute-start | bytes 589832 | tf_op jit(solution)/shard_map/ppermute | solution.py:21
  99.9 9.4 %collective-permute-start.11 = (bf16[768,128]{1,0:T(8,128)(2,1)S(1)}, bf16[768,128]{1,0:T(8,128)(2,1)S(1)}, u32[]{:S(2)}, u32[]{:S(2)}) collective-permute-start(bf16[768,128]{1,0:T(8,128)(2,1)S(1)} %fusion.10), channel_id=1, source_target_pairs={{0,3},{1,2},{2,1},{3,0},{4,7},{5,6},{6,5},{7,4},{8,11},{9,10},{10,... | collective-permute-start | bytes 589832 | tf_op jit(solution)/shard_map/ppermute | solution.py:21
  109.3 1.9 %collective-permute-start.9 = (bf16[768,128]{1,0:T(8,128)(2,1)S(1)}, bf16[768,128]{1,0:T(8,128)(2,1)S(1)}, u32[]{:S(2)}, u32[]{:S(2)}) collective-permute-start(bf16[768,128]{1,0:T(8,128)(2,1)S(1)} %fusion.10), channel_id=1, source_target_pairs={{0,1},{1,0},{2,3},{3,2},{4,5},{5,4},{6,7},{7,6},{8,9},{9,8},{10,11... | collective-permute-start | bytes 589832 | tf_op jit(solution)/shard_map/ppermute | solution.py:21
  111.3 0.0 collective-permute-done.10
  111.3 5.5 %collective-permute-done.11 = bf16[768,128]{1,0:T(8,128)(2,1)S(1)} collective-permute-done((bf16[768,128]{1,0:T(8,128)(2,1)S(1)}, bf16[768,128]{1,0:T(8,128)(2,1)S(1)}, u32[]{:S(2)}, u32[]{:S(2)}) %collective-permute-start.11) | collective-permute-done | bytes 196640 | tf_op jit(solution)/shard_map/ppermute | solution.py:21
  116.8 4.5 %collective-permute-done.9 = bf16[768,128]{1,0:T(8,128)(2,1)S(1)} collective-permute-done((bf16[768,128]{1,0:T(8,128)(2,1)S(1)}, bf16[768,128]{1,0:T(8,128)(2,1)S(1)}, u32[]{:S(2)}, u32[]{:S(2)}) %collective-permute-start.9) | collective-permute-done | bytes 196640 | tf_op jit(solution)/shard_map/ppermute | solution.py:21
  121.3 1.1 all-gather.2.cloned.1.call-done
  122.4 0.0 copy-start
  122.4 3.0 %fusion.51 = (bf16[512,128]{1,0:T(8,128)(2,1)S(1)}, f32[512,128]{1,0:T(8,128)S(1)}) fusion(bf16[768,128]{1,0:T(8,128)(2,1)S(1)} %collective-permute-done.11, bf16[768,128]{1,0:T(8,128)(2,1)S(1)} %collective-permute-done.10, bf16[768,128]{1,0:T(8,128)(2,1)S(1)} %collective-permute-done.9, bf16[768,128]{1,0:T(8,128)(2,1)S(1)} %fusion.10, ...), kind=kOutput, calls=%fused_computation.80 | convolution fusion | flops 405864448 | bytes 4325376 | tf_op jit(solution)/shard_map/dot_general | solution.py:113
  125.4 7.4 %collective-permute-start.13 = (bf16[512,128]{1,0:T(8,128)(2,1)S(1)}, bf16[512,128]{1,0:T(8,128)(2,1)S(1)}, u32[]{:S(2)}, u32[]{:S(2)}) collective-permute-start(bf16[512,128]{1,0:T(8,128)(2,1)S(1)} %get-tuple-element.42), channel_id=1, source_target_pairs={{0,4},{1,5},{2,6},{3,7},{4,0},{5,1},{6,2},{7,3},{8,12},{9,13},{10,... | collective-permute-start | bytes 393224 | tf_op jit(solution)/shard_map/ppermute | solution.py:21
  132.8 0.0 copy-done
  132.8 1.0 fusion.52
  133.9 1.9 %collective-permute-start.12 = (bf16[512,128]{1,0:T(8,128)(2,1)S(1)}, bf16[512,128]{1,0:T(8,128)(2,1)S(1)}, u32[]{:S(2)}, u32[]{:S(2)}) collective-permute-start(bf16[512,128]{1,0:T(8,128)(2,1)S(1)} %get-tuple-element.44), channel_id=1, source_target_pairs={{0,4},{1,5},{2,6},{3,7},{4,0},{5,1},{6,2},{7,3},{8,12},{9,13},{10,... | collective-permute-start | bytes 393224 | tf_op jit(solution)/shard_map/ppermute | solution.py:21
  135.8 17.4 %collective-permute-done.13 = bf16[512,128]{1,0:T(8,128)(2,1)S(1)} collective-permute-done((bf16[512,128]{1,0:T(8,128)(2,1)S(1)}, bf16[512,128]{1,0:T(8,128)(2,1)S(1)}, u32[]{:S(2)}, u32[]{:S(2)}) %collective-permute-start.13) | collective-permute-done | bytes 131104 | tf_op jit(solution)/shard_map/ppermute | solution.py:21
  153.1 1.0 fusion
  154.1 1.8 collective-permute-done.12
  155.9 1.0 fusion.53
  157.0 1.9 %collective-permute-start.14 = (bf16[768,128]{1,0:T(8,128)(2,1)S(1)}, bf16[768,128]{1,0:T(8,128)(2,1)S(1)}, u32[]{:S(2)}, u32[]{:S(2)}) collective-permute-start(bf16[768,128]{1,0:T(8,128)(2,1)S(1)} %get-tuple-element.25), channel_id=1, source_target_pairs={{0,1},{1,0},{2,3},{3,2},{4,5},{5,4},{6,7},{7,6},{8,9},{9,8},{10,11... | collective-permute-start | bytes 589832 | tf_op jit(solution)/shard_map/ppermute | solution.py:21
  158.9 4.9 %collective-permute-start.15 = (bf16[768,128]{1,0:T(8,128)(2,1)S(1)}, bf16[768,128]{1,0:T(8,128)(2,1)S(1)}, u32[]{:S(2)}, u32[]{:S(2)}) collective-permute-start(bf16[768,128]{1,0:T(8,128)(2,1)S(1)} %get-tuple-element.27), channel_id=1, source_target_pairs={{0,2},{1,3},{2,0},{3,1},{4,6},{5,7},{6,4},{7,5},{8,10},{9,11},{10,... | collective-permute-start | bytes 589832 | tf_op jit(solution)/shard_map/ppermute | solution.py:21
  163.8 2.4 %collective-permute-start.16 = (bf16[768,128]{1,0:T(8,128)(2,1)S(1)}, bf16[768,128]{1,0:T(8,128)(2,1)S(1)}, u32[]{:S(2)}, u32[]{:S(2)}) collective-permute-start(bf16[768,128]{1,0:T(8,128)(2,1)S(1)} %get-tuple-element.26), channel_id=1, source_target_pairs={{0,3},{1,2},{2,1},{3,0},{4,7},{5,6},{6,5},{7,4},{8,11},{9,10},{10,... | collective-permute-start | bytes 589832 | tf_op jit(solution)/shard_map/ppermute | solution.py:21
  166.3 0.0 collective-permute-done.14
  166.3 10.5 %collective-permute-done.15 = bf16[768,128]{1,0:T(8,128)(2,1)S(1)} collective-permute-done((bf16[768,128]{1,0:T(8,128)(2,1)S(1)}, bf16[768,128]{1,0:T(8,128)(2,1)S(1)}, u32[]{:S(2)}, u32[]{:S(2)}) %collective-permute-start.15) | collective-permute-done | bytes 196640 | tf_op jit(solution)/shard_map/ppermute | solution.py:21
  176.8 0.0 collective-permute-done.16
  176.8 0.9 fusion.9
  (11 shorter events, 0.3 us)
Async XLA Ops:
  6.5 115.8 %all-gather.2.cloned.1.call-start = ((), (), s32[]{:S(2)}) async-start(), calls=%async_computation.1 | async-start | bytes 6488064 | tf_op jit(solution)/shard_map/all_gather | solution.py:86
  6.5 36.7 %collective-permute-start = (bf16[96,512]{1,0:T(8,128)(2,1)}, bf16[96,512]{1,0:T(8,128)(2,1)S(1)}, u32[]{:S(2)}, u32[]{:S(2)}) collective-permute-start(bf16[96,512]{1,0:T(8,128)(2,1)} %param.8), channel_id=1, source_target_pairs={{0,0},{1,129},{2,258},{3,387},{4,64},{5,193},{6,322},{7,451},{64,1... | collective-permute-start | bytes 294920 | tf_op jit(solution)/shard_map/ppermute | solution.py:21
  8.1 35.2 %collective-permute-start.1 = (bf16[96,512]{1,0:T(8,128)(2,1)}, bf16[96,512]{1,0:T(8,128)(2,1)S(1)}, u32[]{:S(2)}, u32[]{:S(2)}) collective-permute-start(bf16[96,512]{1,0:T(8,128)(2,1)} %param.8), channel_id=1, source_target_pairs={{0,64},{1,193},{2,322},{3,451},{4,0},{5,129},{6,258},{7,387},{64,1... | collective-permute-start | bytes 294920 | tf_op jit(solution)/shard_map/ppermute | solution.py:21
  24.7 14.6 %collective-permute-start.2 = (bf16[96,256]{1,0:T(8,128)(2,1)}, bf16[96,256]{1,0:T(8,128)(2,1)S(1)}, u32[]{:S(2)}, u32[]{:S(2)}) collective-permute-start(bf16[96,256]{1,0:T(8,128)(2,1)} %bitcast.86), channel_id=1, source_target_pairs={{0,0},{1,64},{2,128},{3,192},{4,256},{5,320},{6,384},{7,448},{64,1... | collective-permute-start | bytes 147464 | tf_op jit(solution)/shard_map/ppermute | solution.py:21
  26.2 17.0 %collective-permute-start.3 = (bf16[96,256]{1,0:T(8,128)(2,1)}, bf16[96,256]{1,0:T(8,128)(2,1)S(1)}, u32[]{:S(2)}, u32[]{:S(2)}) collective-permute-start(bf16[96,256]{1,0:T(8,128)(2,1)} %bitcast.87), channel_id=1, source_target_pairs={{0,64},{1,0},{2,192},{3,128},{4,320},{5,256},{6,448},{7,384},{64,6... | collective-permute-start | bytes 147464 | tf_op jit(solution)/shard_map/ppermute | solution.py:21
  47.4 8.9 %collective-permute-start.4 = (bf16[256,128]{1,0:T(8,128)(2,1)S(1)}, bf16[256,128]{1,0:T(8,128)(2,1)S(1)}, u32[]{:S(2)}, u32[]{:S(2)}) collective-permute-start(bf16[256,128]{1,0:T(8,128)(2,1)S(1)} %pad_maximum_fusion.9), channel_id=1, source_target_pairs={{0,4},{1,5},{2,6},{3,7},{4,0},{5,1},{6,2},{7,3},{8,12},{9,13},{10,... | collective-permute-start | bytes 196616 | tf_op jit(solution)/shard_map/ppermute | solution.py:21
  57.6 34.1 %all-to-all-start = ((bf16[16,96,512]{2,1,0:T(8,128)(2,1)}), bf16[16,96,512]{2,1,0:T(8,128)(2,1)S(1)}, u32[]{:S(2)}, u32[]{:S(2)}) async-start(bf16[16,96,512]{2,1,0:T(8,128)(2,1)} %broadcast_in_dim.9), calls=%async_computation | async-start | bytes 3145728 | tf_op jit(solution)/shard_map/all_to_all | solution.py:70
  67.0 7.0 %collective-permute-start.5 = (bf16[2,256,128]{2,1,0:T(8,128)(2,1)S(1)}, bf16[2,256,128]{2,1,0:T(8,128)(2,1)S(1)}, u32[]{:S(2)}, u32[]{:S(2)}) collective-permute-start(bf16[2,256,128]{2,1,0:T(8,128)(2,1)S(1)} %get-tuple-element.35), channel_id=1, source_target_pairs={{0,2},{1,3},{2,0},{3,1},{4,6},{5,7},{6,4},{7,5},{8,10},{9,11},{10,... | collective-permute-start | bytes 393224 | tf_op jit(solution)/shard_map/ppermute | solution.py:21
  74.1 12.0 %collective-permute-start.6 = (bf16[2,2,256,128]{3,2,1,0:T(8,128)(2,1)S(1)}, bf16[2,2,256,128]{3,2,1,0:T(8,128)(2,1)S(1)}, u32[]{:S(2)}, u32[]{:S(2)}) collective-permute-start(bf16[2,2,256,128]{3,2,1,0:T(8,128)(2,1)S(1)} %get-tuple-element.31), channel_id=1, source_target_pairs={{0,1},{1,0},{2,3},{3,2},{4,5},{5,4},{6,7},{7,6},{8,9},{9,8},{10,11... | collective-permute-start | bytes 786440 | tf_op jit(solution)/shard_map/ppermute | solution.py:21
  86.1 5.6 %collective-permute-start.7 = (bf16[4,512,128]{2,1,0:T(8,128)(2,1)S(1)}, bf16[4,512,128]{2,1,0:T(8,128)(2,1)S(1)}, u32[]{:S(2)}, u32[]{:S(2)}) collective-permute-start(bf16[4,512,128]{2,1,0:T(8,128)(2,1)S(1)} %bitcast.75), channel_id=1, source_target_pairs={{0,8},{8,0},{1,9},{9,1},{2,10},{10,2},{3,11},{11,3},{4,12},{12,4},... | collective-permute-start | bytes 1572872 | tf_op jit(solution)/shard_map/ppermute | solution.py:21
  92.8 4.4 %collective-permute-start.8 = (f32[4,1,96,128]{3,2,0,1:T(8,128)S(1)}, f32[4,1,96,128]{3,2,0,1:T(8,128)S(1)}, u32[]{:S(2)}, u32[]{:S(2)}) collective-permute-start(f32[4,1,96,128]{3,2,0,1:T(8,128)S(1)} %bitcast.83), channel_id=1, source_target_pairs={{0,8},{8,0},{1,9},{9,1},{2,10},{10,2},{3,11},{11,3},{4,12},{12,4},... | collective-permute-start | bytes 589832 | tf_op jit(solution)/shard_map/ppermute | solution.py:21
  96.9 1.0 copy-start.1
  97.9 13.3 %collective-permute-start.10 = (bf16[768,128]{1,0:T(8,128)(2,1)S(1)}, bf16[768,128]{1,0:T(8,128)(2,1)S(1)}, u32[]{:S(2)}, u32[]{:S(2)}) collective-permute-start(bf16[768,128]{1,0:T(8,128)(2,1)S(1)} %fusion.10), channel_id=1, source_target_pairs={{0,2},{1,3},{2,0},{3,1},{4,6},{5,7},{6,4},{7,5},{8,10},{9,11},{10,... | collective-permute-start | bytes 589832 | tf_op jit(solution)/shard_map/ppermute | solution.py:21
  99.9 16.8 %collective-permute-start.11 = (bf16[768,128]{1,0:T(8,128)(2,1)S(1)}, bf16[768,128]{1,0:T(8,128)(2,1)S(1)}, u32[]{:S(2)}, u32[]{:S(2)}) collective-permute-start(bf16[768,128]{1,0:T(8,128)(2,1)S(1)} %fusion.10), channel_id=1, source_target_pairs={{0,3},{1,2},{2,1},{3,0},{4,7},{5,6},{6,5},{7,4},{8,11},{9,10},{10,... | collective-permute-start | bytes 589832 | tf_op jit(solution)/shard_map/ppermute | solution.py:21
  109.3 11.9 %collective-permute-start.9 = (bf16[768,128]{1,0:T(8,128)(2,1)S(1)}, bf16[768,128]{1,0:T(8,128)(2,1)S(1)}, u32[]{:S(2)}, u32[]{:S(2)}) collective-permute-start(bf16[768,128]{1,0:T(8,128)(2,1)S(1)} %fusion.10), channel_id=1, source_target_pairs={{0,1},{1,0},{2,3},{3,2},{4,5},{5,4},{6,7},{7,6},{8,9},{9,8},{10,11... | collective-permute-start | bytes 589832 | tf_op jit(solution)/shard_map/ppermute | solution.py:21
  122.4 10.4 %copy-start = (bf16[3072,1024]{1,0:T(8,128)(2,1)S(1)}, bf16[3072,1024]{1,0:T(8,128)(2,1)}, u32[]{:S(2)}) copy-start(bf16[3072,1024]{1,0:T(8,128)(2,1)} %all-gather.2.cloned.1.call-done) | copy-start | bytes 18874372
  125.4 27.7 %collective-permute-start.13 = (bf16[512,128]{1,0:T(8,128)(2,1)S(1)}, bf16[512,128]{1,0:T(8,128)(2,1)S(1)}, u32[]{:S(2)}, u32[]{:S(2)}) collective-permute-start(bf16[512,128]{1,0:T(8,128)(2,1)S(1)} %get-tuple-element.42), channel_id=1, source_target_pairs={{0,4},{1,5},{2,6},{3,7},{4,0},{5,1},{6,2},{7,3},{8,12},{9,13},{10,... | collective-permute-start | bytes 393224 | tf_op jit(solution)/shard_map/ppermute | solution.py:21
  133.9 22.1 %collective-permute-start.12 = (bf16[512,128]{1,0:T(8,128)(2,1)S(1)}, bf16[512,128]{1,0:T(8,128)(2,1)S(1)}, u32[]{:S(2)}, u32[]{:S(2)}) collective-permute-start(bf16[512,128]{1,0:T(8,128)(2,1)S(1)} %get-tuple-element.44), channel_id=1, source_target_pairs={{0,4},{1,5},{2,6},{3,7},{4,0},{5,1},{6,2},{7,3},{8,12},{9,13},{10,... | collective-permute-start | bytes 393224 | tf_op jit(solution)/shard_map/ppermute | solution.py:21
  157.0 9.3 %collective-permute-start.14 = (bf16[768,128]{1,0:T(8,128)(2,1)S(1)}, bf16[768,128]{1,0:T(8,128)(2,1)S(1)}, u32[]{:S(2)}, u32[]{:S(2)}) collective-permute-start(bf16[768,128]{1,0:T(8,128)(2,1)S(1)} %get-tuple-element.25), channel_id=1, source_target_pairs={{0,1},{1,0},{2,3},{3,2},{4,5},{5,4},{6,7},{7,6},{8,9},{9,8},{10,11... | collective-permute-start | bytes 589832 | tf_op jit(solution)/shard_map/ppermute | solution.py:21
  158.9 17.9 %collective-permute-start.15 = (bf16[768,128]{1,0:T(8,128)(2,1)S(1)}, bf16[768,128]{1,0:T(8,128)(2,1)S(1)}, u32[]{:S(2)}, u32[]{:S(2)}) collective-permute-start(bf16[768,128]{1,0:T(8,128)(2,1)S(1)} %get-tuple-element.27), channel_id=1, source_target_pairs={{0,2},{1,3},{2,0},{3,1},{4,6},{5,7},{6,4},{7,5},{8,10},{9,11},{10,... | collective-permute-start | bytes 589832 | tf_op jit(solution)/shard_map/ppermute | solution.py:21
  163.8 13.0 %collective-permute-start.16 = (bf16[768,128]{1,0:T(8,128)(2,1)S(1)}, bf16[768,128]{1,0:T(8,128)(2,1)S(1)}, u32[]{:S(2)}, u32[]{:S(2)}) collective-permute-start(bf16[768,128]{1,0:T(8,128)(2,1)S(1)} %get-tuple-element.26), channel_id=1, source_target_pairs={{0,3},{1,2},{2,1},{3,0},{4,7},{5,6},{6,5},{7,4},{8,11},{9,10},{10,... | collective-permute-start | bytes 589832 | tf_op jit(solution)/shard_map/ppermute | solution.py:21
Sparse Core Ops, SparseCore 0:
  44.1 78.2 all-gather.1

commit v5 on v4

--- a/solution.py
+++ b/solution.py
@@ -44,7 +44,7 @@
 
 
 def act_target(s):
-    return lambda y, h, z: ((z >> 1) ^ y, (z & 1) ^ s, 2 * y + h)
+    return lambda y, h, z: ((z ^ (2 * y + h)) & 3, (z >> 2) ^ s, 2 * y + h)
 
 
 def ordered(flag, first, second, axis):
@@ -85,12 +85,12 @@
     strip = ordered(half == 1, b0, b1, 1)
     panel = lax.all_gather(strip, ("y", "x", "core"), axis=0, tiled=True)
 
-    act_strip = ordered((half ^ (z & 1)) == 1, a0, a1, 1)
+    act_strip = ordered((half ^ (z >> 2)) == 1, a0, a1, 1)
     act_strip, grad, g4 = fence((act_strip, grad, g4))
     act_all = spread(act_strip).reshape(4, -1, act_strip.shape[1])
     g = jnp.stack([grad, g4], axis=0)
-    g = jnp.stack([g, swap_z(g, 1)], axis=1)
-    g = jnp.stack([g, swap_z(g, 0)], axis=2)
+    g = jnp.stack([g, swap_z(g, 1)], axis=0)
+    g = jnp.stack([g, swap_z(g, 0)], axis=1)
     g = g.reshape(4, -1, width)
     g_other = swap_core(g)
     act_all, g, g_other = fence((act_all, g, g_other))

time: 188 us -> 188 us (level)
  waiting for transfers between devices: 63.4 us -> 70.5 us
  starting transfers between devices: 92.1 us -> 85.1 us
    ppermute x17, starting transfers between devices: 82.7 us -> 74.6 us  [routed(): lax.ppermute(value, axes, [(flat[c], flat[tuple(target(*c))]) for c in co...]
    ppermute x17, waiting for transfers between devices: 62.2 us -> 69.1 us  [routed(): lax.ppermute(value, axes, [(flat[c], flat[tuple(target(*c))]) for c in co...]
  transfers between devices with their start and end apart: 19 -> 19, of which waited for: 11 -> 12; matrix products, arithmetic and copies ran while one was open for 5% -> 5% of each run, Pallas kernels for 0% -> 0%
where the time goes in v5:
time: 188 us; the launch traced here: 185 us
  starting transfers between devices  85.1 us (45%)
  waiting for transfers between devices  70.5 us (38%)
  between operations  13.8 us (7%)
  matrix products  8.08 us (4%)
  other arithmetic  3.87 us (2%)
  local copies, waits for them, and re-layouts  3.31 us (2%)
    ppermute x17, starting transfers between devices, routed(): lax.ppermute(value, axes, [(flat[c], flat[tuple(target(*c))]) for c in co...  74.6 us
    ppermute x17, waiting for transfers between devices, routed(): lax.ppermute(value, axes, [(flat[c], flat[tuple(target(*c))]) for c in co...  69.1 us
    all_to_all x1, starting transfers between devices, spread(): return lax.all_to_all(copies, ('y', 'x'), 0, 0)  10.5 us
    dot_general x2, matrix products, project(): lax.dot_general(left, wide, (((0,), (0,)), ((), ())), preferred_element_t...  4.08 us
  transfers between devices with their start and end apart: 19, of which 12 were waited for; matrix products, arithmetic and copies ran while one was open for 5% of the time, Pallas kernels for 0%

profile of v5, /device:TPU:1, one launch (start us, length us, event | category | flops | bytes accessed | tf_op | source)
XLA Modules:
  0.0 184.7 jit_solution(13974671163579024934)
XLA Ops:
  6.5 0.0 all-gather.2.cloned.1.call-start
  6.5 1.5 collective-permute-start
  8.1 16.6 %collective-permute-start.1 = (bf16[96,512]{1,0:T(8,128)(2,1)}, bf16[96,512]{1,0:T(8,128)(2,1)S(1)}, u32[]{:S(2)}, u32[]{:S(2)}) collective-permute-start(bf16[96,512]{1,0:T(8,128)(2,1)} %param.8), channel_id=1, source_target_pairs={{0,64},{1,193},{2,322},{3,451},{4,0},{5,129},{6,258},{7,387},{64,1... | collective-permute-start | bytes 294920 | tf_op jit(solution)/shard_map/ppermute | solution.py:21
  24.7 1.5 collective-permute-start.2
  26.2 14.8 %collective-permute-start.3 = (bf16[96,256]{1,0:T(8,128)(2,1)}, bf16[96,256]{1,0:T(8,128)(2,1)S(1)}, u32[]{:S(2)}, u32[]{:S(2)}) collective-permute-start(bf16[96,256]{1,0:T(8,128)(2,1)} %bitcast.85), channel_id=1, source_target_pairs={{0,64},{1,192},{2,320},{3,448},{4,0},{5,128},{6,256},{7,384},{64,1... | collective-permute-start | bytes 147464 | tf_op jit(solution)/shard_map/ppermute | solution.py:21
  41.0 0.0 collective-permute-done.2
  41.1 1.9 %collective-permute-done.3 = bf16[96,256]{1,0:T(8,128)(2,1)S(1)} collective-permute-done((bf16[96,256]{1,0:T(8,128)(2,1)}, bf16[96,256]{1,0:T(8,128)(2,1)S(1)}, u32[]{:S(2)}, u32[]{:S(2)}) %collective-permute-start.3) | collective-permute-done | bytes 49184 | tf_op jit(solution)/shard_map/ppermute | solution.py:21
  42.9 0.0 collective-permute-done
  42.9 0.0 collective-permute-done.1
  43.0 0.7 pad_maximum_fusion.4
  43.6 0.0 all-gather.2.cloned.1.call-update
  43.7 1.3 fusion.50
  45.0 1.2 iota_compare_fusion
  46.2 0.9 slice_select_fusion.1
  47.1 1.9 %collective-permute-start.4 = (bf16[256,128]{1,0:T(8,128)(2,1)S(1)}, bf16[256,128]{1,0:T(8,128)(2,1)S(1)}, u32[]{:S(2)}, u32[]{:S(2)}) collective-permute-start(bf16[256,128]{1,0:T(8,128)(2,1)S(1)} %pad_maximum_fusion.9), channel_id=1, source_target_pairs={{0,4},{1,5},{2,6},{3,7},{4,0},{5,1},{6,2},{7,3},{8,12},{9,13},{10,... | collective-permute-start | bytes 196616 | tf_op jit(solution)/shard_map/ppermute | solution.py:21
  49.1 7.9 %collective-permute-done.4 = bf16[256,128]{1,0:T(8,128)(2,1)S(1)} collective-permute-done((bf16[256,128]{1,0:T(8,128)(2,1)S(1)}, bf16[256,128]{1,0:T(8,128)(2,1)S(1)}, u32[]{:S(2)}, u32[]{:S(2)}) %collective-permute-start.4) | collective-permute-done | bytes 65568 | tf_op jit(solution)/shard_map/ppermute | solution.py:21
  56.9 1.3 broadcast_in_dim.9
  58.2 10.5 %all-to-all-start = ((bf16[16,96,512]{2,1,0:T(8,128)(2,1)}), bf16[16,96,512]{2,1,0:T(8,128)(2,1)S(1)}, u32[]{:S(2)}, u32[]{:S(2)}) async-start(bf16[16,96,512]{2,1,0:T(8,128)(2,1)} %broadcast_in_dim.9), calls=%async_computation | async-start | bytes 3145728 | tf_op jit(solution)/shard_map/all_to_all | solution.py:70
  68.8 1.9 %collective-permute-start.5 = (bf16[2,256,128]{2,1,0:T(8,128)(2,1)S(1)}, bf16[2,256,128]{2,1,0:T(8,128)(2,1)S(1)}, u32[]{:S(2)}, u32[]{:S(2)}) collective-permute-start(bf16[2,256,128]{2,1,0:T(8,128)(2,1)S(1)} %get-tuple-element.35), channel_id=1, source_target_pairs={{0,2},{1,3},{2,0},{3,1},{4,6},{5,7},{6,4},{7,5},{8,10},{9,11},{10,... | collective-permute-start | bytes 393224 | tf_op jit(solution)/shard_map/ppermute | solution.py:21
  70.8 8.1 %collective-permute-done.5 = bf16[2,256,128]{2,1,0:T(8,128)(2,1)S(1)} collective-permute-done((bf16[2,256,128]{2,1,0:T(8,128)(2,1)S(1)}, bf16[2,256,128]{2,1,0:T(8,128)(2,1)S(1)}, u32[]{:S(2)}, u32[]{:S(2)}) %collective-permute-start.5) | collective-permute-done | bytes 131104 | tf_op jit(solution)/shard_map/ppermute | solution.py:21
  78.9 1.9 %collective-permute-start.6 = (bf16[2,2,256,128]{3,2,1,0:T(8,128)(2,1)S(1)}, bf16[2,2,256,128]{3,2,1,0:T(8,128)(2,1)S(1)}, u32[]{:S(2)}, u32[]{:S(2)}) collective-permute-start(bf16[2,2,256,128]{3,2,1,0:T(8,128)(2,1)S(1)} %get-tuple-element.31), channel_id=1, source_target_pairs={{0,1},{1,0},{2,3},{3,2},{4,5},{5,4},{6,7},{7,6},{8,9},{9,8},{10,11... | collective-permute-start | bytes 786440 | tf_op jit(solution)/shard_map/ppermute | solution.py:21
  80.8 6.8 %collective-permute-done.6 = bf16[2,2,256,128]{3,2,1,0:T(8,128)(2,1)S(1)} collective-permute-done((bf16[2,2,256,128]{3,2,1,0:T(8,128)(2,1)S(1)}, bf16[2,2,256,128]{3,2,1,0:T(8,128)(2,1)S(1)}, u32[]{:S(2)}, u32[]{:S(2)}) %collective-permute-start.6) | collective-permute-done | bytes 262176 | tf_op jit(solution)/shard_map/ppermute | solution.py:21
  87.7 0.1 pad_maximum_fusion.1
  87.7 3.8 %collective-permute-start.7 = (bf16[4,512,128]{2,1,0:T(8,128)(2,1)S(1)}, bf16[4,512,128]{2,1,0:T(8,128)(2,1)S(1)}, u32[]{:S(2)}, u32[]{:S(2)}) collective-permute-start(bf16[4,512,128]{2,1,0:T(8,128)(2,1)S(1)} %bitcast.73), channel_id=1, source_target_pairs={{0,8},{8,0},{1,9},{9,1},{2,10},{10,2},{3,11},{11,3},{4,12},{12,4},... | collective-permute-start | bytes 1572872 | tf_op jit(solution)/shard_map/ppermute | solution.py:21
  91.5 1.5 collective-permute-done.7
  93.0 0.6 all-to-all-done
  93.6 0.3 fusion.19
  93.8 0.3 convolution_add_fusion.6
  94.1 0.3 convolution_add_fusion.5
  94.3 0.3 convolution_add_fusion.4
  94.6 3.7 %collective-permute-start.8 = (f32[4,1,96,128]{3,2,0,1:T(8,128)S(1)}, f32[4,1,96,128]{3,2,0,1:T(8,128)S(1)}, u32[]{:S(2)}, u32[]{:S(2)}) collective-permute-start(f32[4,1,96,128]{3,2,0,1:T(8,128)S(1)} %bitcast.81), channel_id=1, source_target_pairs={{0,8},{8,0},{1,9},{9,1},{2,10},{10,2},{3,11},{11,3},{4,12},{12,4},... | collective-permute-start | bytes 589832 | tf_op jit(solution)/shard_map/ppermute | solution.py:21
  98.3 0.3 fusion.17
  98.5 0.3 convolution_add_fusion.3
  98.8 0.3 convolution_add_fusion.2
  99.1 0.0 copy-start.1
  99.1 0.3 convolution_add_fusion.1
  99.3 0.0 collective-permute-done.8
  99.5 0.6 copy-done.1
  100.1 1.9 %collective-permute-start.10 = (bf16[768,128]{1,0:T(8,128)(2,1)S(1)}, bf16[768,128]{1,0:T(8,128)(2,1)S(1)}, u32[]{:S(2)}, u32[]{:S(2)}) collective-permute-start(bf16[768,128]{1,0:T(8,128)(2,1)S(1)} %fusion.10), channel_id=1, source_target_pairs={{0,2},{1,3},{2,0},{3,1},{4,6},{5,7},{6,4},{7,5},{8,10},{9,11},{10,... | collective-permute-start | bytes 589832 | tf_op jit(solution)/shard_map/ppermute | solution.py:21
  102.0 3.6 %collective-permute-start.11 = (bf16[768,128]{1,0:T(8,128)(2,1)S(1)}, bf16[768,128]{1,0:T(8,128)(2,1)S(1)}, u32[]{:S(2)}, u32[]{:S(2)}) collective-permute-start(bf16[768,128]{1,0:T(8,128)(2,1)S(1)} %fusion.10), channel_id=1, source_target_pairs={{0,3},{1,2},{2,1},{3,0},{4,7},{5,6},{6,5},{7,4},{8,11},{9,10},{10,... | collective-permute-start | bytes 589832 | tf_op jit(solution)/shard_map/ppermute | solution.py:21
  105.6 2.9 %collective-permute-start.9 = (bf16[768,128]{1,0:T(8,128)(2,1)S(1)}, bf16[768,128]{1,0:T(8,128)(2,1)S(1)}, u32[]{:S(2)}, u32[]{:S(2)}) collective-permute-start(bf16[768,128]{1,0:T(8,128)(2,1)S(1)} %fusion.10), channel_id=1, source_target_pairs={{0,1},{1,0},{2,3},{3,2},{4,5},{5,4},{6,7},{7,6},{8,9},{9,8},{10,11... | collective-permute-start | bytes 589832 | tf_op jit(solution)/shard_map/ppermute | solution.py:21
  108.5 9.2 %collective-permute-done.10 = bf16[768,128]{1,0:T(8,128)(2,1)S(1)} collective-permute-done((bf16[768,128]{1,0:T(8,128)(2,1)S(1)}, bf16[768,128]{1,0:T(8,128)(2,1)S(1)}, u32[]{:S(2)}, u32[]{:S(2)}) %collective-permute-start.10) | collective-permute-done | bytes 196640 | tf_op jit(solution)/shard_map/ppermute | solution.py:21
  117.7 0.0 collective-permute-done.11
  117.7 4.0 %collective-permute-done.9 = bf16[768,128]{1,0:T(8,128)(2,1)S(1)} collective-permute-done((bf16[768,128]{1,0:T(8,128)(2,1)S(1)}, bf16[768,128]{1,0:T(8,128)(2,1)S(1)}, u32[]{:S(2)}, u32[]{:S(2)}) %collective-permute-start.9) | collective-permute-done | bytes 196640 | tf_op jit(solution)/shard_map/ppermute | solution.py:21
  121.7 0.8 all-gather.2.cloned.1.call-done
  122.5 0.0 copy-start
  122.5 3.0 %fusion.51 = (bf16[512,128]{1,0:T(8,128)(2,1)S(1)}, f32[512,128]{1,0:T(8,128)S(1)}) fusion(bf16[768,128]{1,0:T(8,128)(2,1)S(1)} %collective-permute-done.11, bf16[768,128]{1,0:T(8,128)(2,1)S(1)} %collective-permute-done.10, bf16[768,128]{1,0:T(8,128)(2,1)S(1)} %collective-permute-done.9, bf16[768,128]{1,0:T(8,128)(2,1)S(1)} %fusion.10, ...), kind=kOutput, calls=%fused_computation.80 | convolution fusion | flops 405864448 | bytes 4325376 | tf_op jit(solution)/shard_map/dot_general | solution.py:113
  125.6 7.4 %collective-permute-start.13 = (bf16[512,128]{1,0:T(8,128)(2,1)S(1)}, bf16[512,128]{1,0:T(8,128)(2,1)S(1)}, u32[]{:S(2)}, u32[]{:S(2)}) collective-permute-start(bf16[512,128]{1,0:T(8,128)(2,1)S(1)} %get-tuple-element.42), channel_id=1, source_target_pairs={{0,4},{1,5},{2,6},{3,7},{4,0},{5,1},{6,2},{7,3},{8,12},{9,13},{10,... | collective-permute-start | bytes 393224 | tf_op jit(solution)/shard_map/ppermute | solution.py:21
  133.0 0.0 copy-done
  133.0 1.0 fusion.52
  134.0 1.9 %collective-permute-start.12 = (bf16[512,128]{1,0:T(8,128)(2,1)S(1)}, bf16[512,128]{1,0:T(8,128)(2,1)S(1)}, u32[]{:S(2)}, u32[]{:S(2)}) collective-permute-start(bf16[512,128]{1,0:T(8,128)(2,1)S(1)} %get-tuple-element.44), channel_id=1, source_target_pairs={{0,4},{1,5},{2,6},{3,7},{4,0},{5,1},{6,2},{7,3},{8,12},{9,13},{10,... | collective-permute-start | bytes 393224 | tf_op jit(solution)/shard_map/ppermute | solution.py:21
  135.9 17.3 %collective-permute-done.13 = bf16[512,128]{1,0:T(8,128)(2,1)S(1)} collective-permute-done((bf16[512,128]{1,0:T(8,128)(2,1)S(1)}, bf16[512,128]{1,0:T(8,128)(2,1)S(1)}, u32[]{:S(2)}, u32[]{:S(2)}) %collective-permute-start.13) | collective-permute-done | bytes 131104 | tf_op jit(solution)/shard_map/ppermute | solution.py:21
  153.3 1.0 fusion
  154.3 1.8 collective-permute-done.12
  156.1 1.0 fusion.53
  157.1 1.9 %collective-permute-start.14 = (bf16[768,128]{1,0:T(8,128)(2,1)S(1)}, bf16[768,128]{1,0:T(8,128)(2,1)S(1)}, u32[]{:S(2)}, u32[]{:S(2)}) collective-permute-start(bf16[768,128]{1,0:T(8,128)(2,1)S(1)} %get-tuple-element.25), channel_id=1, source_target_pairs={{0,1},{1,0},{2,3},{3,2},{4,5},{5,4},{6,7},{7,6},{8,9},{9,8},{10,11... | collective-permute-start | bytes 589832 | tf_op jit(solution)/shard_map/ppermute | solution.py:21
  159.0 4.9 %collective-permute-start.15 = (bf16[768,128]{1,0:T(8,128)(2,1)S(1)}, bf16[768,128]{1,0:T(8,128)(2,1)S(1)}, u32[]{:S(2)}, u32[]{:S(2)}) collective-permute-start(bf16[768,128]{1,0:T(8,128)(2,1)S(1)} %get-tuple-element.27), channel_id=1, source_target_pairs={{0,2},{1,3},{2,0},{3,1},{4,6},{5,7},{6,4},{7,5},{8,10},{9,11},{10,... | collective-permute-start | bytes 589832 | tf_op jit(solution)/shard_map/ppermute | solution.py:21
  164.0 2.4 %collective-permute-start.16 = (bf16[768,128]{1,0:T(8,128)(2,1)S(1)}, bf16[768,128]{1,0:T(8,128)(2,1)S(1)}, u32[]{:S(2)}, u32[]{:S(2)}) collective-permute-start(bf16[768,128]{1,0:T(8,128)(2,1)S(1)} %get-tuple-element.26), channel_id=1, source_target_pairs={{0,3},{1,2},{2,1},{3,0},{4,7},{5,6},{6,5},{7,4},{8,11},{9,10},{10,... | collective-permute-start | bytes 589832 | tf_op jit(solution)/shard_map/ppermute | solution.py:21
  166.4 0.0 collective-permute-done.14
  166.4 10.6 %collective-permute-done.15 = bf16[768,128]{1,0:T(8,128)(2,1)S(1)} collective-permute-done((bf16[768,128]{1,0:T(8,128)(2,1)S(1)}, bf16[768,128]{1,0:T(8,128)(2,1)S(1)}, u32[]{:S(2)}, u32[]{:S(2)}) %collective-permute-start.15) | collective-permute-done | bytes 196640 | tf_op jit(solution)/shard_map/ppermute | solution.py:21
  177.0 0.0 collective-permute-done.16
  177.0 0.9 fusion.9
  (11 shorter events, 0.3 us)
Async XLA Ops:
  6.5 116.0 %all-gather.2.cloned.1.call-start = ((), (), s32[]{:S(2)}) async-start(), calls=%async_computation.1 | async-start | bytes 6488064 | tf_op jit(solution)/shard_map/all_gather | solution.py:86
  6.5 36.4 %collective-permute-start = (bf16[96,512]{1,0:T(8,128)(2,1)}, bf16[96,512]{1,0:T(8,128)(2,1)S(1)}, u32[]{:S(2)}, u32[]{:S(2)}) collective-permute-start(bf16[96,512]{1,0:T(8,128)(2,1)} %param.8), channel_id=1, source_target_pairs={{0,0},{1,129},{2,258},{3,387},{4,64},{5,193},{6,322},{7,451},{64,1... | collective-permute-start | bytes 294920 | tf_op jit(solution)/shard_map/ppermute | solution.py:21
  8.1 34.9 %collective-permute-start.1 = (bf16[96,512]{1,0:T(8,128)(2,1)}, bf16[96,512]{1,0:T(8,128)(2,1)S(1)}, u32[]{:S(2)}, u32[]{:S(2)}) collective-permute-start(bf16[96,512]{1,0:T(8,128)(2,1)} %param.8), channel_id=1, source_target_pairs={{0,64},{1,193},{2,322},{3,451},{4,0},{5,129},{6,258},{7,387},{64,1... | collective-permute-start | bytes 294920 | tf_op jit(solution)/shard_map/ppermute | solution.py:21
  24.7 16.3 %collective-permute-start.2 = (bf16[96,256]{1,0:T(8,128)(2,1)}, bf16[96,256]{1,0:T(8,128)(2,1)S(1)}, u32[]{:S(2)}, u32[]{:S(2)}) collective-permute-start(bf16[96,256]{1,0:T(8,128)(2,1)} %bitcast.84), channel_id=1, source_target_pairs={{0,0},{1,128},{2,256},{3,384},{4,64},{5,192},{6,320},{7,448},{64,1... | collective-permute-start | bytes 147464 | tf_op jit(solution)/shard_map/ppermute | solution.py:21
  26.2 16.7 %collective-permute-start.3 = (bf16[96,256]{1,0:T(8,128)(2,1)}, bf16[96,256]{1,0:T(8,128)(2,1)S(1)}, u32[]{:S(2)}, u32[]{:S(2)}) collective-permute-start(bf16[96,256]{1,0:T(8,128)(2,1)} %bitcast.85), channel_id=1, source_target_pairs={{0,64},{1,192},{2,320},{3,448},{4,0},{5,128},{6,256},{7,384},{64,1... | collective-permute-start | bytes 147464 | tf_op jit(solution)/shard_map/ppermute | solution.py:21
  47.1 9.9 %collective-permute-start.4 = (bf16[256,128]{1,0:T(8,128)(2,1)S(1)}, bf16[256,128]{1,0:T(8,128)(2,1)S(1)}, u32[]{:S(2)}, u32[]{:S(2)}) collective-permute-start(bf16[256,128]{1,0:T(8,128)(2,1)S(1)} %pad_maximum_fusion.9), channel_id=1, source_target_pairs={{0,4},{1,5},{2,6},{3,7},{4,0},{5,1},{6,2},{7,3},{8,12},{9,13},{10,... | collective-permute-start | bytes 196616 | tf_op jit(solution)/shard_map/ppermute | solution.py:21
  58.2 35.3 %all-to-all-start = ((bf16[16,96,512]{2,1,0:T(8,128)(2,1)}), bf16[16,96,512]{2,1,0:T(8,128)(2,1)S(1)}, u32[]{:S(2)}, u32[]{:S(2)}) async-start(bf16[16,96,512]{2,1,0:T(8,128)(2,1)} %broadcast_in_dim.9), calls=%async_computation | async-start | bytes 3145728 | tf_op jit(solution)/shard_map/all_to_all | solution.py:70
  68.8 10.0 %collective-permute-start.5 = (bf16[2,256,128]{2,1,0:T(8,128)(2,1)S(1)}, bf16[2,256,128]{2,1,0:T(8,128)(2,1)S(1)}, u32[]{:S(2)}, u32[]{:S(2)}) collective-permute-start(bf16[2,256,128]{2,1,0:T(8,128)(2,1)S(1)} %get-tuple-element.35), channel_id=1, source_target_pairs={{0,2},{1,3},{2,0},{3,1},{4,6},{5,7},{6,4},{7,5},{8,10},{9,11},{10,... | collective-permute-start | bytes 393224 | tf_op jit(solution)/shard_map/ppermute | solution.py:21
  78.9 8.8 %collective-permute-start.6 = (bf16[2,2,256,128]{3,2,1,0:T(8,128)(2,1)S(1)}, bf16[2,2,256,128]{3,2,1,0:T(8,128)(2,1)S(1)}, u32[]{:S(2)}, u32[]{:S(2)}) collective-permute-start(bf16[2,2,256,128]{3,2,1,0:T(8,128)(2,1)S(1)} %get-tuple-element.31), channel_id=1, source_target_pairs={{0,1},{1,0},{2,3},{3,2},{4,5},{5,4},{6,7},{7,6},{8,9},{9,8},{10,11... | collective-permute-start | bytes 786440 | tf_op jit(solution)/shard_map/ppermute | solution.py:21
  87.7 5.3 %collective-permute-start.7 = (bf16[4,512,128]{2,1,0:T(8,128)(2,1)S(1)}, bf16[4,512,128]{2,1,0:T(8,128)(2,1)S(1)}, u32[]{:S(2)}, u32[]{:S(2)}) collective-permute-start(bf16[4,512,128]{2,1,0:T(8,128)(2,1)S(1)} %bitcast.73), channel_id=1, source_target_pairs={{0,8},{8,0},{1,9},{9,1},{2,10},{10,2},{3,11},{11,3},{4,12},{12,4},... | collective-permute-start | bytes 1572872 | tf_op jit(solution)/shard_map/ppermute | solution.py:21
  94.6 4.7 %collective-permute-start.8 = (f32[4,1,96,128]{3,2,0,1:T(8,128)S(1)}, f32[4,1,96,128]{3,2,0,1:T(8,128)S(1)}, u32[]{:S(2)}, u32[]{:S(2)}) collective-permute-start(f32[4,1,96,128]{3,2,0,1:T(8,128)S(1)} %bitcast.81), channel_id=1, source_target_pairs={{0,8},{8,0},{1,9},{9,1},{2,10},{10,2},{3,11},{11,3},{4,12},{12,4},... | collective-permute-start | bytes 589832 | tf_op jit(solution)/shard_map/ppermute | solution.py:21
  99.1 1.0 copy-start.1
  100.1 17.6 %collective-permute-start.10 = (bf16[768,128]{1,0:T(8,128)(2,1)S(1)}, bf16[768,128]{1,0:T(8,128)(2,1)S(1)}, u32[]{:S(2)}, u32[]{:S(2)}) collective-permute-start(bf16[768,128]{1,0:T(8,128)(2,1)S(1)} %fusion.10), channel_id=1, source_target_pairs={{0,2},{1,3},{2,0},{3,1},{4,6},{5,7},{6,4},{7,5},{8,10},{9,11},{10,... | collective-permute-start | bytes 589832 | tf_op jit(solution)/shard_map/ppermute | solution.py:21
  102.0 15.7 %collective-permute-start.11 = (bf16[768,128]{1,0:T(8,128)(2,1)S(1)}, bf16[768,128]{1,0:T(8,128)(2,1)S(1)}, u32[]{:S(2)}, u32[]{:S(2)}) collective-permute-start(bf16[768,128]{1,0:T(8,128)(2,1)S(1)} %fusion.10), channel_id=1, source_target_pairs={{0,3},{1,2},{2,1},{3,0},{4,7},{5,6},{6,5},{7,4},{8,11},{9,10},{10,... | collective-permute-start | bytes 589832 | tf_op jit(solution)/shard_map/ppermute | solution.py:21
  105.6 16.1 %collective-permute-start.9 = (bf16[768,128]{1,0:T(8,128)(2,1)S(1)}, bf16[768,128]{1,0:T(8,128)(2,1)S(1)}, u32[]{:S(2)}, u32[]{:S(2)}) collective-permute-start(bf16[768,128]{1,0:T(8,128)(2,1)S(1)} %fusion.10), channel_id=1, source_target_pairs={{0,1},{1,0},{2,3},{3,2},{4,5},{5,4},{6,7},{7,6},{8,9},{9,8},{10,11... | collective-permute-start | bytes 589832 | tf_op jit(solution)/shard_map/ppermute | solution.py:21
  122.5 10.4 %copy-start = (bf16[3072,1024]{1,0:T(8,128)(2,1)S(1)}, bf16[3072,1024]{1,0:T(8,128)(2,1)}, u32[]{:S(2)}) copy-start(bf16[3072,1024]{1,0:T(8,128)(2,1)} %all-gather.2.cloned.1.call-done) | copy-start | bytes 18874372
  125.6 27.7 %collective-permute-start.13 = (bf16[512,128]{1,0:T(8,128)(2,1)S(1)}, bf16[512,128]{1,0:T(8,128)(2,1)S(1)}, u32[]{:S(2)}, u32[]{:S(2)}) collective-permute-start(bf16[512,128]{1,0:T(8,128)(2,1)S(1)} %get-tuple-element.42), channel_id=1, source_target_pairs={{0,4},{1,5},{2,6},{3,7},{4,0},{5,1},{6,2},{7,3},{8,12},{9,13},{10,... | collective-permute-start | bytes 393224 | tf_op jit(solution)/shard_map/ppermute | solution.py:21
  134.0 22.1 %collective-permute-start.12 = (bf16[512,128]{1,0:T(8,128)(2,1)S(1)}, bf16[512,128]{1,0:T(8,128)(2,1)S(1)}, u32[]{:S(2)}, u32[]{:S(2)}) collective-permute-start(bf16[512,128]{1,0:T(8,128)(2,1)S(1)} %get-tuple-element.44), channel_id=1, source_target_pairs={{0,4},{1,5},{2,6},{3,7},{4,0},{5,1},{6,2},{7,3},{8,12},{9,13},{10,... | collective-permute-start | bytes 393224 | tf_op jit(solution)/shard_map/ppermute | solution.py:21
  157.1 9.3 %collective-permute-start.14 = (bf16[768,128]{1,0:T(8,128)(2,1)S(1)}, bf16[768,128]{1,0:T(8,128)(2,1)S(1)}, u32[]{:S(2)}, u32[]{:S(2)}) collective-permute-start(bf16[768,128]{1,0:T(8,128)(2,1)S(1)} %get-tuple-element.25), channel_id=1, source_target_pairs={{0,1},{1,0},{2,3},{3,2},{4,5},{5,4},{6,7},{7,6},{8,9},{9,8},{10,11... | collective-permute-start | bytes 589832 | tf_op jit(solution)/shard_map/ppermute | solution.py:21
  159.0 17.9 %collective-permute-start.15 = (bf16[768,128]{1,0:T(8,128)(2,1)S(1)}, bf16[768,128]{1,0:T(8,128)(2,1)S(1)}, u32[]{:S(2)}, u32[]{:S(2)}) collective-permute-start(bf16[768,128]{1,0:T(8,128)(2,1)S(1)} %get-tuple-element.27), channel_id=1, source_target_pairs={{0,2},{1,3},{2,0},{3,1},{4,6},{5,7},{6,4},{7,5},{8,10},{9,11},{10,... | collective-permute-start | bytes 589832 | tf_op jit(solution)/shard_map/ppermute | solution.py:21
  164.0 13.0 %collective-permute-start.16 = (bf16[768,128]{1,0:T(8,128)(2,1)S(1)}, bf16[768,128]{1,0:T(8,128)(2,1)S(1)}, u32[]{:S(2)}, u32[]{:S(2)}) collective-permute-start(bf16[768,128]{1,0:T(8,128)(2,1)S(1)} %get-tuple-element.26), channel_id=1, source_target_pairs={{0,3},{1,2},{2,1},{3,0},{4,7},{5,6},{6,5},{7,4},{8,11},{9,10},{10,... | collective-permute-start | bytes 589832 | tf_op jit(solution)/shard_map/ppermute | solution.py:21
Sparse Core Ops, SparseCore 0:
  43.8 78.6 all-gather.1
